TPU v7x, 512 devices: a whole 4x4x16 slice. The times are simulated.
512 devices in a mesh: wide: 32 (over x, y, core), narrow: 16 (over z).
Axes of the slice: x: 4, y: 4, z: 16, core: 2. Of those that a mesh axis runs over, the one named last changes fastest.
Arguments:
- activations: bfloat16 [65536, 4096], P(('wide', 'narrow')), may hold values from -24 to 24
- grad_gate: bfloat16 [65536, 7168], P(('wide', 'narrow')), may hold values from -24 to 24
- grad_up: bfloat16 [65536, 7168], P(('wide', 'narrow')), may hold values from -24 to 24
- state_gate: float32 [7168, 64], P(('wide', 'narrow')), may hold values from -6 to 6
- state_up: float32 [7168, 64], P(('wide', 'narrow')), may hold values from -6 to 6
Outputs:
- left_gate: float32 [4096, 64], P(('wide', 'narrow'))
- right_gate: float32 [7168, 64], P(('wide', 'narrow'))
- left_up: float32 [4096, 64], P(('wide', 'narrow'))
- right_up: float32 [7168, 64], P(('wide', 'narrow'))
All inputs are finite; a program needn't handle non-finite values.
Results may differ from a plain program's by a relative error of at most 0.0004.
Values sent between devices are 32-bit elements; how exact they have to be, the bound alone decides.
No kernel may reach another device: no remote copies, remote signals or barrier semaphores. Data moves between devices by JAX's collectives and lax.ppermute only.
A program may use at most 64 MiB of HBM per device.

v0:
```python
import math

import jax
import jax.numpy as jnp
from jax import lax
from jax.sharding import PartitionSpec as P

HIGH = lax.Precision.HIGHEST


def tokens_contract(left, right):
    return lax.dot_general(
        left, right, (((0,), (0,)), ((), ())), precision=HIGH, preferred_element_type=jnp.float32
    )


def local_left(activations, grads, state, factor):
    small = jnp.dot(grads, state, precision=HIGH, preferred_element_type=jnp.float32)
    return tokens_contract(activations, small) * factor


def lower_factor(raw):
    gram = jnp.dot(raw.T, raw, precision=HIGH, preferred_element_type=jnp.float32)
    return jnp.linalg.cholesky(gram)


def orthogonal(raw, lower):
    return lax.linalg.triangular_solve(lower, raw, left_side=False, lower=True, transpose_a=True)


def shards(activations, grad_gate, grad_up, state_gate, state_up):
    devices = lax.axis_size(("wide", "narrow"))
    factor = jnp.float32(1.0 / math.sqrt(activations.shape[0] * devices))
    width = activations.shape[1]
    rank = state_gate.shape[1]
    full_gate, full_up = (
        lax.all_gather(state_gate, ("wide", "narrow"), axis=0, tiled=True),
        lax.all_gather(state_up, ("wide", "narrow"), axis=0, tiled=True),
    )
    raw_gate, raw_up = lax.psum(
        (
            local_left(activations, grad_gate, full_gate, factor),
            local_left(activations, grad_up, full_up, factor),
        ),
        ("wide", "narrow"),
    )
    lower_gate = lower_factor(raw_gate)
    lower_up = lower_factor(raw_up)
    basis_gate = orthogonal(raw_gate, lower_gate)
    basis_up = orthogonal(raw_up, lower_up)
    project_gate = jnp.dot(
        activations, basis_gate, precision=HIGH, preferred_element_type=jnp.float32
    )
    project_up = jnp.dot(activations, basis_up, precision=HIGH, preferred_element_type=jnp.float32)
    joined = jnp.concatenate(
        [tokens_contract(grad_gate, project_gate), tokens_contract(grad_up, project_up)], axis=1
    )
    summed = lax.psum_scatter(joined * factor, ("wide", "narrow"), scatter_dimension=0, tiled=True)
    right_gate = summed[:, :rank]
    right_up = summed[:, rank:]
    rows = width // devices
    start = lax.axis_index(("wide", "narrow")) * rows
    stretch = jnp.float32(math.sqrt(width))
    left_gate = lax.dynamic_slice_in_dim(basis_gate, start, rows, 0) * stretch
    left_up = lax.dynamic_slice_in_dim(basis_up, start, rows, 0) * stretch
    return (left_gate, right_gate, left_up, right_up)


def solution(mesh):
    placed = (
        P(("wide", "narrow"), None),
        P(("wide", "narrow"), None),
        P(("wide", "narrow"), None),
        P(("wide", "narrow"), None),
        P(("wide", "narrow"), None),
    )
    return jax.shard_map(
        shards,
        mesh=mesh,
        in_specs=placed,
        out_specs=(
            P(("wide", "narrow"), None),
            P(("wide", "narrow"), None),
            P(("wide", "narrow"), None),
            P(("wide", "narrow"), None),
        ),
        check_vma=False,
    )
```

profile of v0, /device:TPU:1, one launch (start us, length us, event | category | flops | bytes accessed | tf_op | source)
XLA Modules:
  0.0 1434.0 jit_solution(14745826991420826039)
XLA Ops:
  7.2 0.7 all-gather.5.cloned.1.call-update
  8.0 0.7 all-gather.7.cloned.1.call-update
  8.7 207.4 %all-gather.5.cloned.1.call-done = f32[512,14,64]{2,1,0:T(8,128)} async-done(((f32[1,14,64]{2,1,0:T(8,128)}), f32[512,14,64]{2,1,0:T(8,128)}) %all-gather.5.cloned.1.call-update) | async-done | bytes 1835024 | tf_op jit(solution)/shard_map/all_gather | solution.py:37
  216.1 4.7 reshape.22
  220.8 5.1 fusion.9
  225.9 188.3 %all-gather.7.cloned.1.call-done = f32[512,14,64]{2,1,0:T(8,128)} async-done(((f32[1,14,64]{2,1,0:T(8,128)}), f32[512,14,64]{2,1,0:T(8,128)}) %all-gather.7.cloned.1.call-update) | async-done | bytes 1835024 | tf_op jit(solution)/shard_map/all_gather | solution.py:38
  414.2 4.6 reshape.24
  418.8 5.7 fusion.12
  424.5 1.5 fusion.1
  426.1 1.6 fusion
  427.9 471.5 %all-reduce.7.cloned.1.call-done = (f32[4096,64]{0,1:T(8,128)}, f32[4096,64]{0,1:T(8,128)}) async-done(((f32[4096,64]{0,1:T(8,128)}, f32[4096,64]{0,1:T(8,128)}), (f32[4096,64]{0,1:T(8,128)}, f32[4096,64]{0,1:T(8,128)})) %all-reduce.7.cloned.1.call-update) | async-done | bytes 2097168 | tf_op jit(solution)/shard_map/psum | solution.py:40
  899.4 2.6 fusion.10
  902.0 1.0 fusion.13
  903.1 5.8 cholesky.55
  910.3 4.9 custom-call.7
  915.2 2.3 convolution_bitcast_fusion.2
  917.4 1.0 copy-done.4
  918.4 1.2 fusion.14
  919.7 5.8 cholesky.44
  926.9 4.9 custom-call.6
  931.8 2.3 convolution_bitcast_fusion.3
  934.1 1.0 copy-done.5
  935.1 1.2 fusion.11
  936.3 0.9 convolution_bitcast_fusion.1
  937.8 0.9 convolution_bitcast_fusion
  938.7 2.2 maximum_multiply_fusion
  940.9 0.9 dynamic-slice_multiply_fusion
  941.7 0.7 copy.25
  943.1 482.1 %all-reduce.5.cloned.1.call-done = f32[7168,128]{0,1:T(8,128)} async-done(((f32[7168,128]{0,1:T(8,128)}), f32[7168,128]{0,1:T(8,128)}) %all-reduce.5.cloned.1.call-update) | async-done | bytes 3670032
  1425.2 1.0 fusion.8
  1426.1 0.7 copy.26
  1426.8 0.7 copy.24
  (27 shorter events, 4.5 us)
Async XLA Ops:
  7.2 213.6 %copy-start = (bf16[128,7168]{1,0:T(8,128)(2,1)S(1)}, bf16[128,7168]{1,0:T(8,128)(2,1)}, u32[]{:S(2)}) copy-start(bf16[128,7168]{1,0:T(8,128)(2,1)} %param.9) | copy-start | bytes 5505028
  7.2 208.9 %all-gather.5.cloned.1.call-start = ((), (), s32[]{:S(2)}) async-start(), calls=%async_computation | async-start | bytes 4202496 | tf_op jit(solution)/shard_map/all_gather | solution.py:37
  7.9 406.2 %all-gather.7.cloned.1.call-start = ((), (), s32[]{:S(2)}) async-start(), calls=%async_computation.1 | async-start | bytes 4202496 | tf_op jit(solution)/shard_map/all_gather | solution.py:38
  8.7 890.7 %all-reduce.7.cloned.1.call-start = ((), (), s32[]{:S(2)}) async-start(), calls=%async_computation.3 | async-start | bytes 4194304 | tf_op jit(solution)/shard_map/psum | solution.py:40
  418.8 5.7 copy-start.1
  427.7 997.5 %all-reduce.5.cloned.1.call-start = ((), (), s32[]{:S(2)}) async-start(), calls=%async_computation.2 | async-start | bytes 7340032
  899.4 2.6 copy-start.2
  917.4 1.0 copy-start.4
  934.1 1.0 copy-start.5
  936.3 1.5 copy-start.3
Sparse Core Ops, SparseCore 0:
  12.6 203.4 all-gather.4
  220.7 193.3 all-gather.6
  427.8 471.5 all-reduce.6
  941.0 484.1 all-reduce.4
where the time goes:
time: 1440 us; the launch traced here: 1430 us
  waiting for transfers between devices  1350 us (94%)
  other arithmetic  27.2 us (2%)
  matrix products  26.1 us (2%)
  local copies, waits for them, and re-layouts  15.7 us (1%)
    unnamed x5, waiting for transfers between devices  484 us
    psum x1, waiting for transfers between devices, shards(): lax.psum((local_left(activations, grad_gate, full_gate, factor), local_le...  472 us
    all_gather x1, waiting for transfers between devices, shards(): lax.all_gather(state_gate, ('wide', 'narrow'), axis=0, tiled=True)  207 us
    all_gather x1, waiting for transfers between devices, shards(): lax.all_gather(state_up, ('wide', 'narrow'), axis=0, tiled=True)  188 us
  transfers between devices with their start and end apart: 4, of which 4 were waited for; matrix products, arithmetic and copies ran while one was open for 1% of the time, Pallas kernels for 0%

commit v1 on v0

v1 whole, which is shorter than its diff:
```python
import math

import jax
import jax.numpy as jnp
from jax import lax
from jax.sharding import Mesh, PartitionSpec as P

HIGH = lax.Precision.HIGHEST
PLANE = ("x", "y")
EVERY = ("x", "y", "core", "z")


def parts_of(value):
    first = lax.reduce_precision(value, 8, 7)
    rest = value - first
    second = lax.reduce_precision(rest, 8, 7)
    third = rest - second
    return [piece.astype(jnp.bfloat16) for piece in (first, second, third)]


def exact_dot(left, right, contract):
    columns = right.shape[1]
    joined = jnp.concatenate(parts_of(right), axis=1)
    wide = lax.dot_general(
        left, joined, (((contract,), (0,)), ((), ())), preferred_element_type=jnp.float32
    )
    return wide[:, :columns] + wide[:, columns : 2 * columns] + wide[:, 2 * columns :]


def exchange(value, axes):
    return lax.all_to_all(value, axes, 0, 0, tiled=True)


def spread(block, axes):
    count = lax.axis_size(axes)
    return exchange(jnp.broadcast_to(block[None], (count, *block.shape)), axes)


def other_core(value):
    return lax.ppermute(value, "core", [(0, 1), (1, 0)])


def gather_rows(block):
    rows, columns = block.shape
    line = spread(block, "z").reshape(-1, columns)
    plane = spread(line, PLANE)
    other = other_core(plane)
    first = lax.axis_index("core") == 0
    whole = jnp.stack(
        [jnp.where(first, plane, other), jnp.where(first, other, plane)], axis=1
    )
    return whole.reshape(-1, columns)


def scatter_rows(whole):
    columns = whole.shape[1]
    core = lax.axis_index("core")
    count = lax.axis_size(PLANE)
    lines = whole.reshape(count, 2, -1, columns)
    keep = lax.dynamic_index_in_dim(lines, core, 1, keepdims=False)
    give = lax.dynamic_index_in_dim(lines, 1 - core, 1, keepdims=False)
    chip = keep + other_core(give)
    line = jnp.sum(exchange(chip, PLANE), axis=0)
    stack = line.reshape(lax.axis_size("z"), -1, columns)
    return jnp.sum(exchange(stack, "z"), axis=0)


def shards(activations, grad_gate, grad_up, state_gate, state_up):
    devices = lax.axis_size(EVERY)
    factor = jnp.float32(1.0 / math.sqrt(activations.shape[0] * devices))
    width = activations.shape[1]
    rank = state_gate.shape[1]

    state = gather_rows(jnp.concatenate([state_gate, state_up], axis=1))
    small = jnp.concatenate(
        [exact_dot(grad_gate, state[:, :rank], 1), exact_dot(grad_up, state[:, rank:], 1)],
        axis=1,
    )
    mine = scatter_rows(exact_dot(activations, small, 0)) * factor
    raw = gather_rows(mine)

    project = exact_dot(activations, raw, 1) * factor
    joined = jnp.concatenate(
        [
            exact_dot(grad_gate, project[:, :rank], 0),
            exact_dot(grad_up, project[:, rank:], 0),
        ],
        axis=1,
    )
    summed = scatter_rows(joined)

    gram = lax.dot_general(
        raw, raw, (((0,), (0,)), ((), ())), precision=HIGH, preferred_element_type=jnp.float32
    )
    lower = jnp.linalg.cholesky(
        jnp.stack([gram[:rank, :rank], gram[rank:, rank:]]), symmetrize_input=False
    )
    rows = jnp.concatenate([mine, summed], axis=0)
    rows = jnp.stack([rows[:, :rank], rows[:, rank:]])
    solved = lax.linalg.triangular_solve(
        lower, rows, left_side=False, lower=True, transpose_a=True
    )
    stretch = jnp.float32(math.sqrt(width))
    own = mine.shape[0]
    left = solved[:, :own] * stretch
    right = solved[:, own:]
    return (left[0], right[0], left[1], right[1])


def solution(mesh):
    wide, narrow = mesh.devices.shape
    side = math.isqrt(wide // 2)
    fine = Mesh(mesh.devices.reshape(side, side, 2, narrow), EVERY)
    rows = P(EVERY, None)
    return jax.shard_map(
        shards,
        mesh=fine,
        in_specs=(rows,) * 5,
        out_specs=(rows,) * 4,
        check_vma=False,
    )
```

time: 1440 us -> 259 us (0.18)
  waiting for transfers between devices: 1350 us -> 22.9 us
  blocking collectives: 0 us -> 121 us
  starting transfers between devices: 0.34 us -> 28.2 us
  local copies, waits for them, and re-layouts: 15.7 us -> 33 us
  matrix products: 26.1 us -> 10.7 us
    unnamed x5 -> x0, waiting for transfers between devices: 484 us -> none
    psum x1 -> x0, waiting for transfers between devices: 472 us -> none  [shards(): lax.psum((local_left(activations, grad_gate, full_gate, factor), local_le...]
    all_gather x2 -> x0, waiting for transfers between devices: 396 us -> none  [the longest x1 207 us: shards(): lax.all_gather(state_gate, ('wide', 'narrow'), axis=0, tiled=True)]
    all_to_all x0 -> x6, blocking collectives: none -> 121 us  [exchange(): return lax.all_to_all(value, axes, 0, 0, tiled=True)]
    ppermute x0 -> x4, starting transfers between devices: none -> 20.3 us  [other_core(): return lax.ppermute(value, 'core', [(0, 1), (1, 0)])]
  transfers between devices with their start and end apart: 4 -> 6, of which waited for: 4 -> 6; matrix products, arithmetic and copies ran while one was open for 1% -> 10% of each run, Pallas kernels for 0% -> 0%
where the time goes in v1:
time: 259 us; the launch traced here: 257 us
  blocking collectives  121 us (47%)
  other arithmetic  39.6 us (15%)
  local copies, waits for them, and re-layouts  33 us (13%)
  starting transfers between devices  28.2 us (11%)
  waiting for transfers between devices  22.9 us (9%)
  matrix products  10.7 us (4%)
    all_to_all x6, blocking collectives, exchange(): return lax.all_to_all(value, axes, 0, 0, tiled=True)  121 us
    ppermute x4, starting transfers between devices, other_core(): return lax.ppermute(value, 'core', [(0, 1), (1, 0)])  20.3 us
    another operation x4, other arithmetic, shards(): jnp.linalg.cholesky(jnp.stack([gram[:rank, :rank], gram[rank:, rank:]]),...  11.9 us
    ppermute x4, waiting for transfers between devices, other_core(): return lax.ppermute(value, 'core', [(0, 1), (1, 0)])  11.5 us
    all_to_all x2, waiting for transfers between devices, exchange(): return lax.all_to_all(value, axes, 0, 0, tiled=True)  11.4 us
    unnamed x20, local copies, waits for them, and re-layouts  10.8 us
    another operation x3, other arithmetic, shards(): lax.linalg.triangular_solve(lower, rows, left_side=False, lower=True, tra...  9.92 us
    all_to_all x2, starting transfers between devices, exchange(): return lax.all_to_all(value, axes, 0, 0, tiled=True)  7.93 us
  transfers between devices with their start and end apart: 6, of which 6 were waited for; matrix products, arithmetic and copies ran while one was open for 10% of the time, Pallas kernels for 0%

profile of v1, /device:TPU:1, one launch (start us, length us, event | category | flops | bytes accessed | tf_op | source)
XLA Modules:
  0.0 256.6 jit_solution(5732645395051391900)
XLA Ops:
  1.6 27.5 %all_to_all.40 = f32[16,14,128]{2,1,0:T(8,128)S(1)} all-to-all(f32[16,14,128]{2,1,0:T(8,128)S(1)} %broadcast_in_dim.14), channel_id=1, replica_groups=mesh['x'=4,'y'=4,'core'=2,'z'=16] {'z'}, dimensions={0} | all-to-all | bytes 229376 | tf_op jit(solution)/shard_map/all_to_all | solution.py:31
  29.3 27.6 %all_to_all.41 = f32[16,224,128]{2,1,0:T(8,128)} all-to-all(f32[16,224,128]{2,1,0:T(8,128)S(1)} %broadcast_in_dim.32), channel_id=1, replica_groups=mesh['x'=4,'y'=4,'core'=2,'z'=16] {'x','y'}, dimensions={0} | all-to-all | bytes 3670016 | tf_op jit(solution)/shard_map/all_to_all | solution.py:31
  56.9 7.3 %collective-permute-start = (f32[16,224,128]{2,1,0:T(8,128)}, f32[16,224,128]{2,1,0:T(8,128)}, u32[]{:S(2)}, u32[]{:S(2)}) collective-permute-start(f32[16,224,128]{2,1,0:T(8,128)} %all_to_all.41), channel_id=1, source_target_pairs={{0,16},{16,0},{1,17},{17,1},{2,18},{18,2},{3,19},{19,3},{4,20},{20... | collective-permute-start | bytes 5505032 | tf_op jit(solution)/shard_map/ppermute | solution.py:40
  64.2 3.7 %collective-permute-done = f32[16,224,128]{2,1,0:T(8,128)} collective-permute-done((f32[16,224,128]{2,1,0:T(8,128)}, f32[16,224,128]{2,1,0:T(8,128)}, u32[]{:S(2)}, u32[]{:S(2)}) %collective-permute-start) | collective-permute-done | bytes 1835040 | tf_op jit(solution)/shard_map/ppermute | solution.py:40
  67.9 2.3 select_bitcast_fusion.1
  70.5 4.1 %fusion.62 = (f32[7168,64]{1,0:T(8,128)}, f32[7168,64]{1,0:T(8,128)}) fusion(f32[7168,128]{1,0:T(8,128)S(1)} %bitcast.77), kind=kLoop, calls=%fused_computation.127 | loop fusion | bytes 7340032 | tf_op jit(solution)/shard_map/slice | solution.py:76
  74.6 3.5 %copy.59 = f32[7168,64]{0,1:T(8,128)} copy(f32[7168,64]{1,0:T(8,128)} %get-tuple-element.5) | data formatting | bytes 3670016
  78.1 3.2 %reduce-precision_convert_fusion.3 = (bf16[7168,64]{0,1:T(8,128)(2,1)S(1)}, bf16[7168,64]{0,1:T(8,128)(2,1)}, bf16[7168,64]{0,1:T(8,128)(2,1)}) fusion(f32[7168,64]{0,1:T(8,128)} %copy.59), kind=kLoop, calls=%fused_computation.30 | loop fusion | flops 3211264 | bytes 4587520 | tf_op jit(solution)/shard_map/convert_element_type | solution.py:18
  81.3 3.5 %copy.58 = f32[7168,64]{0,1:T(8,128)} copy(f32[7168,64]{1,0:T(8,128)} %get-tuple-element.4) | data formatting | bytes 3670016
  84.9 2.1 reduce-precision_convert_fusion.5
  92.3 4.0 %reshape.43 = f32[16,2,128,128]{2,1,0,3:T(2,128)} reshape(f32[4096,128]{0,1:T(8,128)} %slice_add_fusion) | data formatting | bytes 4194304 | tf_op jit(solution)/shard_map/reshape | solution.py:59
  96.3 4.4 %constant_dynamic-slice_fusion.1 = (f32[16,1,128,128]{2,1,0,3:T(1,128)S(1)}, f32[16,1,128,128]{2,1,0,3:T(1,128)S(1)}) fusion(f32[16,2,128,128]{2,1,0,3:T(2,128)} %reshape.43, s32[]{:T(128)S(6)} %select_n.41, s32[]{:T(128)S(6)} %select_n.42), kind=kLoop, calls=%fused_computation.119 | loop fusion | bytes 4194312 | tf_op jit(solution)/shard_map/jit(dynamic_index_in_dim)/dynamic_slice | solution.py:60
  101.1 2.3 collective-permute-start.1
  103.4 2.3 collective-permute-done.1
  106.1 19.2 %all_to_all.42 = f32[16,128,128]{1,2,0:T(8,128)S(1)} all-to-all(f32[16,128,128]{1,2,0:T(8,128)S(1)} %bitcast_add_fusion.1), channel_id=1, replica_groups=mesh['x'=4,'y'=4,'core'=2,'z'=16] {'x','y'}, dimensions={0} | all-to-all | bytes 2097152 | tf_op jit(solution)/shard_map/all_to_all | solution.py:31
  125.4 17.3 %all_to_all.43 = f32[16,8,128]{2,1,0:T(8,128)S(1)} all-to-all(f32[16,8,128]{2,1,0:T(8,128)S(1)} %bitcast.82), channel_id=1, replica_groups=mesh['x'=4,'y'=4,'core'=2,'z'=16] {'z'}, dimensions={0} | all-to-all | bytes 131072 | tf_op jit(solution)/shard_map/all_to_all | solution.py:31
  142.8 14.3 %all_to_all.44 = f32[16,8,128]{2,1,0:T(8,128)S(1)} all-to-all(f32[16,8,128]{2,1,0:T(8,128)S(1)} %broadcast_in_dim.33), channel_id=1, replica_groups=mesh['x'=4,'y'=4,'core'=2,'z'=16] {'z'}, dimensions={0} | all-to-all | bytes 131072 | tf_op jit(solution)/shard_map/all_to_all | solution.py:31
  157.2 15.2 %all_to_all.45 = f32[16,128,128]{2,1,0:T(8,128)S(1)} all-to-all(f32[16,128,128]{2,1,0:T(8,128)S(1)} %broadcast_in_dim.35), channel_id=1, replica_groups=mesh['x'=4,'y'=4,'core'=2,'z'=16] {'x','y'}, dimensions={0} | all-to-all | bytes 2097152 | tf_op jit(solution)/shard_map/all_to_all | solution.py:31
  172.4 8.5 %collective-permute-start.2 = (f32[16,128,128]{2,1,0:T(8,128)S(1)}, f32[16,128,128]{2,1,0:T(8,128)S(1)}, u32[]{:S(2)}, u32[]{:S(2)}) collective-permute-start(f32[16,128,128]{2,1,0:T(8,128)S(1)} %all_to_all.45), channel_id=1, source_target_pairs={{0,16},{16,0},{1,17},{17,1},{2,18},{18,2},{3,19},{19,3},{4,20},{20... | collective-permute-start | bytes 3145736 | tf_op jit(solution)/shard_map/ppermute | solution.py:40
  180.9 2.1 collective-permute-done.2
  190.2 2.1 pad_maximum_fusion.1
  192.3 5.3 %copy.51 = f32[7168,128]{1,0:T(8,128)} copy(f32[7168,128]{0,1:T(8,128)} %pad_maximum_fusion.1) | data formatting | bytes 7340032 | tf_op jit(solution)/shard_map/concatenate | solution.py:83
  197.6 1.8 dynamic-slice_bitcast_fusion
  199.4 2.3 collective-permute-start.3
  201.7 3.4 %collective-permute-done.3 = f32[16,224,128]{2,1,0:T(8,128)S(1)} collective-permute-done((f32[16,224,128]{2,1,0:T(8,128)S(1)}, f32[16,224,128]{2,1,0:T(8,128)S(1)}, u32[]{:S(2)}, u32[]{:S(2)}) %collective-permute-start.3) | collective-permute-done | bytes 1835040 | tf_op jit(solution)/shard_map/ppermute | solution.py:40
  206.5 4.4 %all-to-all-start.6 = ((f32[16,224,128]{2,1,0:T(8,128)}), f32[16,224,128]{2,1,0:T(8,128)}, u32[]{:S(2)}, u32[]{:S(2)}) async-start(f32[16,224,128]{2,1,0:T(8,128)} %bitcast_add_fusion), calls=%async_computation.6 | async-start | bytes 3670016 | tf_op jit(solution)/shard_map/all_to_all | solution.py:31
  211.0 5.0 %convolution_bitcast_fusion.3 = f32[128,128]{1,0:T(8,128)S(1)} fusion(f32[16,1,128,128]{3,2,1,0:T(8,128)} %copy-done.2, f32[16,1,128,128]{3,2,1,0:T(8,128)S(1)} %get-tuple-element.11), kind=kOutput, calls=%fused_computation.52 | convolution fusion | flops 805830656 | bytes 2162688 | tf_op jit(solution)/shard_map/dot_general | solution.py:92
  216.1 11.7 %custom-call.7 = f32[2,64,64]{2,1,0:T(8,128)S(1)} custom-call(f32[2,64,64]{2,1,0:T(8,128)S(1)} %pad_maximum_fusion.4), custom_call_target="Cholesky" | custom-call | tf_op jit(solution)/shard_map/jit(cholesky)/cholesky | solution.py:95
  227.8 9.6 %all-to-all-done.6 = f32[16,224,128]{2,1,0:T(8,128)} async-done(((f32[16,224,128]{2,1,0:T(8,128)}), f32[16,224,128]{2,1,0:T(8,128)}, u32[]{:S(2)}, u32[]{:S(2)}) %all-to-all-start.6) | async-done | bytes 1835040 | tf_op jit(solution)/shard_map/all_to_all | solution.py:31
  239.6 3.5 %all-to-all-start.7 = ((f32[16,14,128]{2,1,0:T(8,128)}), f32[16,14,128]{2,1,0:T(8,128)S(1)}, u32[]{:S(2)}, u32[]{:S(2)}) async-start(f32[16,14,128]{2,1,0:T(8,128)} %reshape.47), calls=%async_computation.7 | async-start | bytes 262144 | tf_op jit(solution)/shard_map/all_to_all | solution.py:31
  243.4 9.8 %custom-call.8 = f32[2,1,64,64]{2,3,1,0:T(8,128)S(1)} custom-call(f32[2,1,64,64]{3,2,1,0:T(8,128)S(1)} %select_bitcast_fusion.4), custom_call_target="InvertDiagBlocksLowerTriangular" | custom-call | tf_op jit(solution)/shard_map/triangular_solve | solution.py:100
  253.2 1.9 all-to-all-done.7
  (63 shorter events, 20.4 us)
Async XLA Ops:
  0.6 86.3 %copy-start = (bf16[128,7168]{1,0:T(8,128)(2,1)S(1)}, bf16[128,7168]{1,0:T(8,128)(2,1)}, u32[]{:S(2)}) copy-start(bf16[128,7168]{1,0:T(8,128)(2,1)} %param.7) | copy-start | bytes 5505028
  56.9 11.0 %collective-permute-start = (f32[16,224,128]{2,1,0:T(8,128)}, f32[16,224,128]{2,1,0:T(8,128)}, u32[]{:S(2)}, u32[]{:S(2)}) collective-permute-start(f32[16,224,128]{2,1,0:T(8,128)} %all_to_all.41), channel_id=1, source_target_pairs={{0,16},{16,0},{1,17},{17,1},{2,18},{18,2},{3,19},{19,3},{4,20},{20... | collective-permute-start | bytes 5505032 | tf_op jit(solution)/shard_map/ppermute | solution.py:40
  84.9 2.1 copy-start.7
  84.9 2.1 copy-start.8
  87.0 1.5 copy-start.3
  88.5 1.2 copy-start.5
  101.1 4.6 %collective-permute-start.1 = (f32[16,128,128]{1,2,0:T(8,128)S(1)}, f32[16,128,128]{1,2,0:T(8,128)S(1)}, u32[]{:S(2)}, u32[]{:S(2)}) collective-permute-start(f32[16,128,128]{1,2,0:T(8,128)S(1)} %bitcast.80), channel_id=1, source_target_pairs={{0,16},{16,0},{1,17},{17,1},{2,18},{18,2},{3,19},{19,3},{4,20},{20... | collective-permute-start | bytes 3145736 | tf_op jit(solution)/shard_map/ppermute | solution.py:40
  172.4 10.6 %collective-permute-start.2 = (f32[16,128,128]{2,1,0:T(8,128)S(1)}, f32[16,128,128]{2,1,0:T(8,128)S(1)}, u32[]{:S(2)}, u32[]{:S(2)}) collective-permute-start(f32[16,128,128]{2,1,0:T(8,128)S(1)} %all_to_all.45), channel_id=1, source_target_pairs={{0,16},{16,0},{1,17},{17,1},{2,18},{18,2},{3,19},{19,3},{4,20},{20... | collective-permute-start | bytes 3145736 | tf_op jit(solution)/shard_map/ppermute | solution.py:40
  183.2 1.0 copy-start.2
  184.4 1.2 copy-start.6
  187.6 1.5 copy-start.4
  197.6 7.5 %copy-start.1 = (f32[7168,128]{1,0:T(8,128)S(1)}, f32[7168,128]{1,0:T(8,128)}, u32[]{:S(2)}) copy-start(f32[7168,128]{1,0:T(8,128)} %copy.51) | copy-start | bytes 11010052
  199.4 5.7 %collective-permute-start.3 = (f32[16,224,128]{2,1,0:T(8,128)S(1)}, f32[16,224,128]{2,1,0:T(8,128)S(1)}, u32[]{:S(2)}, u32[]{:S(2)}) collective-permute-start(f32[16,224,128]{2,1,0:T(8,128)S(1)} %dynamic-slice_bitcast_fusion), channel_id=1, source_target_pairs={{0,16},{16,0},{1,17},{17,1},{2,18},{18,2},{3,19},{19,3},{4,20},{20... | collective-permute-start | bytes 5505032 | tf_op jit(solution)/shard_map/ppermute | solution.py:40
  206.5 30.9 %all-to-all-start.6 = ((f32[16,224,128]{2,1,0:T(8,128)}), f32[16,224,128]{2,1,0:T(8,128)}, u32[]{:S(2)}, u32[]{:S(2)}) async-start(f32[16,224,128]{2,1,0:T(8,128)} %bitcast_add_fusion), calls=%async_computation.6 | async-start | bytes 3670016 | tf_op jit(solution)/shard_map/all_to_all | solution.py:31
  239.6 15.4 %all-to-all-start.7 = ((f32[16,14,128]{2,1,0:T(8,128)}), f32[16,14,128]{2,1,0:T(8,128)S(1)}, u32[]{:S(2)}, u32[]{:S(2)}) async-start(f32[16,14,128]{2,1,0:T(8,128)} %reshape.47), calls=%async_computation.7 | async-start | bytes 262144 | tf_op jit(solution)/shard_map/all_to_all | solution.py:31

commit v2 on v1

v2 whole, which is shorter than its diff:
```python
import functools
import math

import jax
import jax.numpy as jnp
from jax import lax
from jax.experimental import pallas as pl
from jax.experimental.pallas import tpu as pltpu
from jax.sharding import Mesh, PartitionSpec as P

HIGH = lax.Precision.HIGHEST
PLANE = ("x", "y")
EVERY = ("x", "y", "core", "z")
PARAMS = pltpu.CompilerParams(vmem_limit_bytes=20 * 1024 * 1024)


def exchange(value, axes):
    return lax.all_to_all(value, axes, 0, 0, tiled=True)


def spread(block, axes):
    count = lax.axis_size(axes)
    return exchange(jnp.broadcast_to(block[None], (count, *block.shape)), axes)


def other_core(value):
    return lax.ppermute(value, "core", [(0, 1), (1, 0)])


def gather_line(block):
    return spread(block, "z").reshape(-1, block.shape[1])


def gather_plane(block):
    return spread(block, PLANE).reshape(-1, block.shape[1])


def scatter_rows(whole):
    columns = whole.shape[1]
    chip = whole.reshape(lax.axis_size(PLANE), -1, columns)
    line = jnp.sum(exchange(chip, PLANE), axis=0)
    stack = line.reshape(lax.axis_size("z"), -1, columns)
    return jnp.sum(exchange(stack, "z"), axis=0)


def in_vmem(kernel, *shapes, first=()):
    single = len(shapes) == 1

    def call(*values):
        places = [*first, *[pltpu.VMEM] * (len(values) - len(first))]
        return pl.pallas_call(
            kernel,
            out_shape=shapes[0] if single else shapes,
            in_specs=[pl.BlockSpec(memory_space=place) for place in places],
            compiler_params=PARAMS,
            cost_estimate=pl.CostEstimate(flops=1, bytes_accessed=1, transcendentals=0),
        )(*values)

    return call


def shape_of(rows, columns, kind=jnp.float32):
    return jax.ShapeDtypeStruct((rows, columns), kind)


def sorted_blocks(core_ref, count, own, value_refs, write):
    def walk(kept):
        place = 0
        for value_ref in value_refs:
            block = value_ref.shape[1] // (2 * count)
            for i in range(count):
                start = (2 * i + kept) * block
                write(value_ref[:, start : start + block], place, place + block)
                place += block

    pl.when(core_ref[0] == (0 if own else 1))(lambda: walk(0))
    pl.when(core_ref[0] == (1 if own else 0))(lambda: walk(1))


def give_kernel(count, core_ref, after_ref, *refs):
    del after_ref
    inputs = 3
    ends = []
    for ref in refs[inputs:]:
        ends.append(ref.shape[1] + (ends[-1] if ends else 0))

    def write(value, start, stop):
        which = next(i for i, end in enumerate(ends) if stop <= end)
        base = ends[which] - refs[inputs + which].shape[1]
        refs[inputs + which][:, start - base : stop - base] = value.astype(jnp.float32)

    sorted_blocks(core_ref, count, False, refs[:inputs], write)


def give(core, after, *values):
    tokens = values[0].shape[0]
    pieces = [1, 2, 2]
    widths = [v.shape[1] // 2 // n for v, n in zip(values, pieces) for _ in range(n)]
    return in_vmem(
        functools.partial(give_kernel, lax.axis_size(PLANE)),
        *[shape_of(tokens, width) for width in widths],
        first=(pltpu.SMEM, pl.ANY),
    )(core.reshape(1), after, *values)


def keep_kernel(count, core_ref, after_ref, *refs):
    del after_ref
    *value_refs, rows_ref, turned_ref = refs

    def write(value, start, stop):
        rows_ref[:, start:stop] = value

    sorted_blocks(core_ref, count, True, value_refs, write)
    turned_ref[...] = rows_ref[...].astype(jnp.float32).T.astype(jnp.bfloat16)


def keep(core, after, *values):
    tokens = values[0].shape[0]
    columns = sum(v.shape[1] for v in values) // 2
    return in_vmem(
        functools.partial(keep_kernel, lax.axis_size(PLANE)),
        shape_of(tokens, columns, jnp.bfloat16),
        shape_of(columns, tokens, jnp.bfloat16),
        first=(pltpu.SMEM, pl.ANY),
    )(core.reshape(1), after, *values)


def merge_kernel(groups, kept_ref, turned_ref, *refs):
    tokens = kept_ref.shape[0]
    pieces, outs = refs[: sum(groups)], refs[sum(groups) :]
    place = 0
    for rows_out, turned_out, count in zip(outs[::2], outs[1::2], groups):
        width = rows_out.shape[1]
        rows_out[:tokens, :] = kept_ref[:, place : place + width]
        turned_out[:, :tokens] = turned_ref[place : place + width, :]
        place += width
        start = 0
        for piece_ref in pieces[:count]:
            to = slice(start, start + piece_ref.shape[1])
            piece = piece_ref[...]
            rows_out[tokens:, to] = piece.astype(jnp.bfloat16)
            turned_out[to, tokens:] = piece.T.astype(jnp.bfloat16)
            start = to.stop
        pieces = pieces[count:]


def merge(kept, turned, pieces, groups):
    tokens = 2 * kept.shape[0]
    shapes, rest = [], list(pieces)
    for count in groups:
        width = sum(p.shape[1] for p in rest[:count])
        rest = rest[count:]
        shapes += [shape_of(tokens, width, jnp.bfloat16), shape_of(width, tokens, jnp.bfloat16)]
    return in_vmem(functools.partial(merge_kernel, groups), *shapes)(kept, turned, *pieces)


def halves(value):
    high = value.astype(jnp.bfloat16)
    low = (value - high.astype(jnp.float32)).astype(jnp.bfloat16)
    return jnp.concatenate([high, low], axis=1)


def fold(value):
    columns = value.shape[1] // 2
    return value[:, :columns] + value[:, columns:]


def product(left, right):
    return fold(jnp.dot(left, right, preferred_element_type=jnp.float32))


def joined(gate, up):
    lane = lax.broadcasted_iota(jnp.int32, gate.shape, 1)
    return jnp.where(lane < gate.shape[1] // 2, gate, up)


def swapped(mine, other):
    tokens = mine.shape[0] // 2
    return jnp.concatenate(
        [mine[:tokens] + other[tokens:], mine[tokens:] + other[:tokens]], axis=0
    )


def small_kernel(rows_ref, state_ref, out_ref):
    state = halves(state_ref[...])
    columns = state.shape[0]
    out_ref[...] = joined(
        product(rows_ref[:, :columns], state),
        product(rows_ref[:, columns:], state),
    )


def raw_kernel(turned_ref, mine_ref, other_ref, out_ref):
    small = halves(swapped(mine_ref[...], other_ref[...]))
    out_ref[...] = product(turned_ref[...], small)


def project_kernel(factor, rows_ref, raw_ref, out_ref):
    out_ref[...] = product(rows_ref[...], halves(raw_ref[...])) * factor


def right_kernel(turned_ref, mine_ref, other_ref, out_ref):
    project = halves(swapped(mine_ref[...], other_ref[...]))
    columns = out_ref.shape[0]
    out_ref[...] = joined(
        product(turned_ref[:columns, :], project),
        product(turned_ref[columns:, :], project),
    )


def shards(activations, grad_gate, grad_up, state_gate, state_up):
    devices = lax.axis_size(EVERY)
    core = lax.axis_index("core")
    tokens, width = activations.shape
    factor = 1.0 / math.sqrt(tokens * devices)
    rank = state_gate.shape[1]
    both = 2 * rank

    line = gather_line(jnp.concatenate([state_gate, state_up], axis=1))
    values = (activations, grad_gate, grad_up)
    taken = [other_core(piece) for piece in give(core, line, *values)]
    kept, turned = keep(core, line, *values)
    state = gather_plane(line)
    act, act_turned, grad, grad_turned = merge(kept, turned, taken, (1, 4))

    small = in_vmem(small_kernel, shape_of(2 * tokens, both))(grad, state)
    partial = in_vmem(raw_kernel, shape_of(width // 2, both))(
        act_turned, small, other_core(small)
    )
    mine = scatter_rows(partial) * jnp.float32(factor)
    raw = gather_plane(gather_line(mine))

    project = in_vmem(
        functools.partial(project_kernel, factor), shape_of(2 * tokens, both)
    )(act, raw)
    partial = in_vmem(right_kernel, shape_of(state.shape[0], both))(
        grad_turned, project, other_core(project)
    )
    summed = scatter_rows(partial)

    gram = lax.dot_general(
        raw, raw, (((0,), (0,)), ((), ())), precision=HIGH, preferred_element_type=jnp.float32
    )
    gram = gram + other_core(gram)
    lower = jnp.linalg.cholesky(
        jnp.stack([gram[:rank, :rank], gram[rank:, rank:]]), symmetrize_input=False
    )
    rows = jnp.concatenate([mine, summed], axis=0)
    rows = jnp.stack([rows[:, :rank], rows[:, rank:]])
    solved = lax.linalg.triangular_solve(
        lower, rows, left_side=False, lower=True, transpose_a=True
    )
    stretch = jnp.float32(math.sqrt(width))
    own = mine.shape[0]
    left = solved[:, :own] * stretch
    right = solved[:, own:]
    return (left[0], right[0], left[1], right[1])


def solution(mesh):
    wide, narrow = mesh.devices.shape
    side = math.isqrt(wide // 2)
    fine = Mesh(mesh.devices.reshape(side, side, 2, narrow), EVERY)
    rows = P(EVERY, None)
    return jax.shard_map(
        shards,
        mesh=fine,
        in_specs=(rows,) * 5,
        out_specs=(rows,) * 4,
        check_vma=False,
    )
```

time: 259 us -> 200 us (0.77)
  blocking collectives: 121 us -> 94.4 us
  local copies, waits for them, and re-layouts: 33 us -> 13.2 us
  other arithmetic: 39.6 us -> 22.9 us
  starting transfers between devices: 28.2 us -> 42.3 us
  matrix products: 10.7 us -> 2 us
  waiting for transfers between devices: 22.9 us -> 14.6 us
  Pallas kernels: 0 us -> 7.78 us
    all_to_all x6 -> x5, blocking collectives: 121 us -> 94.4 us  [exchange(): return lax.all_to_all(value, axes, 0, 0, tiled=True)]
    ppermute x4 -> x8, waiting for transfers between devices: 11.5 us -> 3.36 us  [other_core(): return lax.ppermute(value, 'core', [(0, 1), (1, 0)])]
    pallas_call x0 -> x7, Pallas kernels: none -> 7.78 us  [call(): pl.pallas_call(kernel, out_shape=shapes[0] if single else shapes, in_spec...]
    ppermute x4 -> x8, starting transfers between devices: 20.3 us -> 28.1 us  [other_core(): return lax.ppermute(value, 'core', [(0, 1), (1, 0)])]
    all_to_all x2 -> x3, starting transfers between devices: 7.93 us -> 14.3 us  [exchange(): return lax.all_to_all(value, axes, 0, 0, tiled=True)]
    convert_element_type x5 -> x0, other arithmetic: 5.87 us -> none  [parts_of(): return [piece.astype(jnp.bfloat16) for piece in (first, second, third)]]
    dot_general x6 -> x0, matrix products: 5.5 us -> none  [exact_dot(): lax.dot_general(left, joined, (((contract,), (0,)), ((), ())), preferred_...]
    concatenate x1 -> x0, local copies, waits for them, and re-layouts: 5.27 us -> none  [shards(): jnp.concatenate([exact_dot(grad_gate, project[:, :rank], 0), exact_dot(gr...]
  transfers between devices with their start and end apart: 6 -> 11, of which waited for: 6 -> 6; matrix products, arithmetic and copies ran while one was open for 10% -> 12% of each run, Pallas kernels for 0% -> 2%
where the time goes in v2:
time: 200 us; the launch traced here: 198 us
  blocking collectives  94.4 us (47%)
  starting transfers between devices  42.3 us (21%)
  other arithmetic  22.9 us (11%)
  waiting for transfers between devices  14.6 us (7%)
  local copies, waits for them, and re-layouts  13.2 us (7%)
  Pallas kernels  7.78 us (4%)
  matrix products  2 us (1%)
    all_to_all x5, blocking collectives, exchange(): return lax.all_to_all(value, axes, 0, 0, tiled=True)  94.4 us
    ppermute x8, starting transfers between devices, other_core(): return lax.ppermute(value, 'core', [(0, 1), (1, 0)])  28.1 us
    all_to_all x3, starting transfers between devices, exchange(): return lax.all_to_all(value, axes, 0, 0, tiled=True)  14.3 us
    another operation x4, other arithmetic, shards(): jnp.linalg.cholesky(jnp.stack([gram[:rank, :rank], gram[rank:, rank:]]),...  11.9 us
    all_to_all x3, waiting for transfers between devices, exchange(): return lax.all_to_all(value, axes, 0, 0, tiled=True)  11.2 us
    another operation x3, other arithmetic, shards(): lax.linalg.triangular_solve(lower, rows, left_side=False, lower=True, tra...  9.92 us
    unnamed x18, local copies, waits for them, and re-layouts  9.63 us
    pallas_call x7, Pallas kernels, call(): pl.pallas_call(kernel, out_shape=shapes[0] if single else shapes, in_spec...  7.78 us
  transfers between devices with their start and end apart: 11, of which 6 were waited for; matrix products, arithmetic and copies ran while one was open for 12% of the time, Pallas kernels for 2%

profile of v2, /device:TPU:1, one launch (start us, length us, event | category | flops | bytes accessed | tf_op | source)
XLA Modules:
  0.0 198.0 jit_solution(5501714173339287241)
XLA Ops:
  1.4 27.5 %all_to_all.40 = f32[16,14,128]{2,1,0:T(8,128)S(1)} all-to-all(f32[16,14,128]{2,1,0:T(8,128)S(1)} %broadcast_in_dim.12), channel_id=1, replica_groups=mesh['x'=4,'y'=4,'core'=2,'z'=16] {'z'}, dimensions={0} | all-to-all | bytes 229376 | tf_op jit(solution)/shard_map/all_to_all | solution.py:18
  29.0 1.5 broadcast_in_dim.13
  30.5 6.9 %all-to-all-start.1 = ((f32[16,224,128]{2,1,0:T(8,128)}), f32[16,224,128]{2,1,0:T(8,128)S(1)}, u32[]{:S(2)}, u32[]{:S(2)}) async-start(f32[16,224,128]{2,1,0:T(8,128)} %broadcast_in_dim.13), calls=%async_computation.1 | async-start | bytes 3670016 | tf_op jit(solution)/shard_map/all_to_all | solution.py:18
  37.4 1.5 copy-done
  38.9 1.5 copy-done.1
  41.1 5.8 %collective-permute-start = (f32[128,2048]{1,0:T(8,128)S(1)}, f32[128,2048]{1,0:T(8,128)S(1)}, u32[]{:S(2)}, u32[]{:S(2)}) collective-permute-start(f32[128,2048]{1,0:T(8,128)S(1)} %get-tuple-element.17), channel_id=1, source_target_pairs={{0,16},{16,0},{1,17},{17,1},{2,18},{18,2},{3,19},{19,3},{4,20},{20... | collective-permute-start | bytes 3145736 | tf_op jit(solution)/shard_map/ppermute | solution.py:27
  46.9 1.9 collective-permute-start.1
  48.8 2.4 %collective-permute-start.2 = (f32[128,1792]{1,0:T(8,128)S(1)}, f32[128,1792]{1,0:T(8,128)S(1)}, u32[]{:S(2)}, u32[]{:S(2)}) collective-permute-start(f32[128,1792]{1,0:T(8,128)S(1)} %get-tuple-element.19), channel_id=1, source_target_pairs={{0,16},{16,0},{1,17},{17,1},{2,18},{18,2},{3,19},{19,3},{4,20},{20... | collective-permute-start | bytes 2752520 | tf_op jit(solution)/shard_map/ppermute | solution.py:27
  51.3 1.9 collective-permute-start.3
  53.2 2.4 %collective-permute-start.4 = (f32[128,1792]{1,0:T(8,128)S(1)}, f32[128,1792]{1,0:T(8,128)S(1)}, u32[]{:S(2)}, u32[]{:S(2)}) collective-permute-start(f32[128,1792]{1,0:T(8,128)S(1)} %get-tuple-element.21), channel_id=1, source_target_pairs={{0,16},{16,0},{1,17},{17,1},{2,18},{18,2},{3,19},{19,3},{4,20},{20... | collective-permute-start | bytes 2752520 | tf_op jit(solution)/shard_map/ppermute | solution.py:27
  55.6 1.5 shard_map.84
  57.7 1.2 shard_map.86
  58.9 1.8 copy-done.3
  60.7 1.8 copy-done.5
  63.5 2.0 %copy-done.6 = bf16[256,7168]{1,0:T(8,128)(2,1)S(1)} copy-done((bf16[256,7168]{1,0:T(8,128)(2,1)S(1)}, bf16[256,7168]{1,0:T(8,128)(2,1)}, u32[]{:S(2)}) %copy-start.6) | copy-done | bytes 3670040
  65.6 1.1 shard_map.87.mine_ref
  66.7 3.0 %collective-permute-start.5 = (f32[256,128]{1,0:T(8,128)S(1)}, f32[256,128]{1,0:T(8,128)S(1)}, u32[]{:S(2)}, u32[]{:S(2)}) collective-permute-start(f32[256,128]{1,0:T(8,128)S(1)} %shard_map.87.mine_ref), channel_id=1, source_target_pairs={{0,16},{16,0},{1,17},{17,1},{2,18},{18,2},{3,19},{19,3},{4,20},{20... | collective-permute-start | bytes 393224 | tf_op jit(solution)/shard_map/ppermute | solution.py:27
  71.1 22.0 %all_to_all.41 = f32[16,128,128]{2,1,0:T(8,128)S(1)} all-to-all(f32[16,128,128]{2,1,0:T(8,128)S(1)} %bitcast.34), channel_id=1, replica_groups=mesh['x'=4,'y'=4,'core'=2,'z'=16] {'x','y'}, dimensions={0} | all-to-all | bytes 2097152 | tf_op jit(solution)/shard_map/all_to_all | solution.py:18
  93.2 14.9 %all_to_all.42 = f32[16,8,128]{2,1,0:T(8,128)S(1)} all-to-all(f32[16,8,128]{2,1,0:T(8,128)S(1)} %bitcast.35), channel_id=1, replica_groups=mesh['x'=4,'y'=4,'core'=2,'z'=16] {'z'}, dimensions={0} | all-to-all | bytes 131072 | tf_op jit(solution)/shard_map/all_to_all | solution.py:18
  108.1 14.4 %all_to_all.43 = f32[16,8,128]{2,1,0:T(8,128)S(1)} all-to-all(f32[16,8,128]{2,1,0:T(8,128)S(1)} %broadcast_in_dim.14), channel_id=1, replica_groups=mesh['x'=4,'y'=4,'core'=2,'z'=16] {'z'}, dimensions={0} | all-to-all | bytes 131072 | tf_op jit(solution)/shard_map/all_to_all | solution.py:18
  122.6 15.5 %all_to_all.44 = f32[16,128,128]{2,1,0:T(8,128)S(1)} all-to-all(f32[16,128,128]{2,1,0:T(8,128)S(1)} %broadcast_in_dim.32), channel_id=1, replica_groups=mesh['x'=4,'y'=4,'core'=2,'z'=16] {'x','y'}, dimensions={0} | all-to-all | bytes 2097152 | tf_op jit(solution)/shard_map/all_to_all | solution.py:18
  138.6 8.3 %collective-permute-start.6 = (f32[256,128]{1,0:T(8,128)S(1)}, f32[256,128]{1,0:T(8,128)S(1)}, u32[]{:S(2)}, u32[]{:S(2)}) collective-permute-start(f32[256,128]{1,0:T(8,128)S(1)} %shard_map.89.mine_ref), channel_id=1, source_target_pairs={{0,16},{16,0},{1,17},{17,1},{2,18},{18,2},{3,19},{19,3},{4,20},{20... | collective-permute-start | bytes 393224 | tf_op jit(solution)/shard_map/ppermute | solution.py:27
  146.9 1.0 collective-permute-done.6.other_ref
  147.8 2.4 %shard_map.90 = f32[3584,128]{1,0:T(8,128)} custom-call(bf16[7168,256]{1,0:T(8,128)(2,1)S(1)} %copy-done.4, f32[256,128]{1,0:T(8,128)S(1)} %shard_map.89.mine_ref, f32[256,128]{1,0:T(8,128)S(1)} %collective-permute-done.6.other_ref), custom_call_target="tpu_custom_call" | custom-call | flops 1 | bytes 1 | tf_op jit(solution)/shard_map/pallas_call | solution.py:51
  150.2 3.9 %all-to-all-start.6 = ((f32[16,224,128]{2,1,0:T(8,128)}), f32[16,224,128]{2,1,0:T(8,128)S(1)}, u32[]{:S(2)}, u32[]{:S(2)}) async-start(f32[16,224,128]{2,1,0:T(8,128)} %bitcast.6), calls=%async_computation.6 | async-start | bytes 3670016 | tf_op jit(solution)/shard_map/all_to_all | solution.py:18
  154.1 1.8 convolution_bitcast_fusion
  156.0 2.3 %collective-permute-start.7 = (f32[128,128]{1,0:T(8,128)S(1)}, f32[128,128]{1,0:T(8,128)S(1)}, u32[]{:S(2)}, u32[]{:S(2)}) collective-permute-start(f32[128,128]{1,0:T(8,128)S(1)} %convolution_bitcast_fusion), channel_id=1, source_target_pairs={{0,16},{16,0},{1,17},{17,1},{2,18},{18,2},{3,19},{19,3},{4,20},{20... | collective-permute-start | bytes 196616 | tf_op jit(solution)/shard_map/ppermute | solution.py:27
  159.2 11.7 %custom-call.7 = f32[2,64,64]{2,1,0:T(8,128)S(1)} custom-call(f32[2,64,64]{2,1,0:T(8,128)S(1)} %pad_maximum_fusion), custom_call_target="Cholesky" | custom-call | tf_op jit(solution)/shard_map/jit(cholesky)/cholesky | solution.py:245
  171.0 9.4 %all-to-all-done.6 = f32[16,224,128]{2,1,0:T(8,128)S(1)} async-done(((f32[16,224,128]{2,1,0:T(8,128)}), f32[16,224,128]{2,1,0:T(8,128)S(1)}, u32[]{:S(2)}, u32[]{:S(2)}) %all-to-all-start.6) | async-done | bytes 1835040 | tf_op jit(solution)/shard_map/all_to_all | solution.py:18
  181.1 3.5 %all-to-all-start.7 = ((f32[16,14,128]{2,1,0:T(8,128)}), f32[16,14,128]{2,1,0:T(8,128)S(1)}, u32[]{:S(2)}, u32[]{:S(2)}) async-start(f32[16,14,128]{2,1,0:T(8,128)} %reshape.56), calls=%async_computation.7 | async-start | bytes 262144 | tf_op jit(solution)/shard_map/all_to_all | solution.py:18
  184.8 9.8 %custom-call.8 = f32[2,1,64,64]{2,3,1,0:T(8,128)S(1)} custom-call(f32[2,1,64,64]{3,2,1,0:T(8,128)S(1)} %select_bitcast_fusion), custom_call_target="InvertDiagBlocksLowerTriangular" | custom-call | tf_op jit(solution)/shard_map/triangular_solve | solution.py:250
  194.7 1.9 all-to-all-done.7
  (48 shorter events, 8.5 us)
Async XLA Ops:
  30.5 6.9 %copy-start.2 = (bf16[128,4096]{1,0:T(8,128)(2,1)S(1)}, bf16[128,4096]{1,0:T(8,128)(2,1)}, u32[]{:S(2)}) copy-start(bf16[128,4096]{1,0:T(8,128)(2,1)} %refs_0_.3) | copy-start | bytes 3145732
  30.5 33.1 %all-to-all-start.1 = ((f32[16,224,128]{2,1,0:T(8,128)}), f32[16,224,128]{2,1,0:T(8,128)S(1)}, u32[]{:S(2)}, u32[]{:S(2)}) async-start(f32[16,224,128]{2,1,0:T(8,128)} %broadcast_in_dim.13), calls=%async_computation.1 | async-start | bytes 3670016 | tf_op jit(solution)/shard_map/all_to_all | solution.py:18
  37.4 1.5 copy-start
  38.9 1.5 copy-start.1
  41.1 16.6 %collective-permute-start = (f32[128,2048]{1,0:T(8,128)S(1)}, f32[128,2048]{1,0:T(8,128)S(1)}, u32[]{:S(2)}, u32[]{:S(2)}) collective-permute-start(f32[128,2048]{1,0:T(8,128)S(1)} %get-tuple-element.17), channel_id=1, source_target_pairs={{0,16},{16,0},{1,17},{17,1},{2,18},{18,2},{3,19},{19,3},{4,20},{20... | collective-permute-start | bytes 3145736 | tf_op jit(solution)/shard_map/ppermute | solution.py:27
  46.9 10.2 %collective-permute-start.1 = (f32[128,1792]{1,0:T(8,128)S(1)}, f32[128,1792]{1,0:T(8,128)S(1)}, u32[]{:S(2)}, u32[]{:S(2)}) collective-permute-start(f32[128,1792]{1,0:T(8,128)S(1)} %get-tuple-element.18), channel_id=1, source_target_pairs={{0,16},{16,0},{1,17},{17,1},{2,18},{18,2},{3,19},{19,3},{4,20},{20... | collective-permute-start | bytes 2752520 | tf_op jit(solution)/shard_map/ppermute | solution.py:27
  48.8 8.3 %collective-permute-start.2 = (f32[128,1792]{1,0:T(8,128)S(1)}, f32[128,1792]{1,0:T(8,128)S(1)}, u32[]{:S(2)}, u32[]{:S(2)}) collective-permute-start(f32[128,1792]{1,0:T(8,128)S(1)} %get-tuple-element.19), channel_id=1, source_target_pairs={{0,16},{16,0},{1,17},{17,1},{2,18},{18,2},{3,19},{19,3},{4,20},{20... | collective-permute-start | bytes 2752520 | tf_op jit(solution)/shard_map/ppermute | solution.py:27
  51.3 5.9 %collective-permute-start.3 = (f32[128,1792]{1,0:T(8,128)S(1)}, f32[128,1792]{1,0:T(8,128)S(1)}, u32[]{:S(2)}, u32[]{:S(2)}) collective-permute-start(f32[128,1792]{1,0:T(8,128)S(1)} %get-tuple-element.20), channel_id=1, source_target_pairs={{0,16},{16,0},{1,17},{17,1},{2,18},{18,2},{3,19},{19,3},{4,20},{20... | collective-permute-start | bytes 2752520 | tf_op jit(solution)/shard_map/ppermute | solution.py:27
  53.2 4.5 %collective-permute-start.4 = (f32[128,1792]{1,0:T(8,128)S(1)}, f32[128,1792]{1,0:T(8,128)S(1)}, u32[]{:S(2)}, u32[]{:S(2)}) collective-permute-start(f32[128,1792]{1,0:T(8,128)S(1)} %get-tuple-element.21), channel_id=1, source_target_pairs={{0,16},{16,0},{1,17},{17,1},{2,18},{18,2},{3,19},{19,3},{4,20},{20... | collective-permute-start | bytes 2752520 | tf_op jit(solution)/shard_map/ppermute | solution.py:27
  58.9 1.8 copy-start.3
  60.7 1.8 copy-start.5
  62.6 1.0 copy-start.7
  63.5 2.0 %copy-start.6 = (bf16[256,7168]{1,0:T(8,128)(2,1)S(1)}, bf16[256,7168]{1,0:T(8,128)(2,1)}, u32[]{:S(2)}) copy-start(bf16[256,7168]{1,0:T(8,128)(2,1)} %copy-done.5) | copy-start | bytes 11010052
  65.6 5.1 %copy-start.8 = (bf16[2048,256]{1,0:T(8,128)(2,1)S(1)}, bf16[2048,256]{1,0:T(8,128)(2,1)}, u32[]{:S(2)}) copy-start(bf16[2048,256]{1,0:T(8,128)(2,1)} %copy-done.7) | copy-start | bytes 3145732
  66.7 4.0 %collective-permute-start.5 = (f32[256,128]{1,0:T(8,128)S(1)}, f32[256,128]{1,0:T(8,128)S(1)}, u32[]{:S(2)}, u32[]{:S(2)}) collective-permute-start(f32[256,128]{1,0:T(8,128)S(1)} %shard_map.87.mine_ref), channel_id=1, source_target_pairs={{0,16},{16,0},{1,17},{17,1},{2,18},{18,2},{3,19},{19,3},{4,20},{20... | collective-permute-start | bytes 393224 | tf_op jit(solution)/shard_map/ppermute | solution.py:27
  122.6 25.2 %copy-start.4 = (bf16[7168,256]{1,0:T(8,128)(2,1)S(1)}, bf16[7168,256]{1,0:T(8,128)(2,1)}, u32[]{:S(2)}) copy-start(bf16[7168,256]{1,0:T(8,128)(2,1)} %copy-done.3) | copy-start | bytes 11010052
  138.6 9.3 %collective-permute-start.6 = (f32[256,128]{1,0:T(8,128)S(1)}, f32[256,128]{1,0:T(8,128)S(1)}, u32[]{:S(2)}, u32[]{:S(2)}) collective-permute-start(f32[256,128]{1,0:T(8,128)S(1)} %shard_map.89.mine_ref), channel_id=1, source_target_pairs={{0,16},{16,0},{1,17},{17,1},{2,18},{18,2},{3,19},{19,3},{4,20},{20... | collective-permute-start | bytes 393224 | tf_op jit(solution)/shard_map/ppermute | solution.py:27
  150.2 30.1 %all-to-all-start.6 = ((f32[16,224,128]{2,1,0:T(8,128)}), f32[16,224,128]{2,1,0:T(8,128)S(1)}, u32[]{:S(2)}, u32[]{:S(2)}) async-start(f32[16,224,128]{2,1,0:T(8,128)} %bitcast.6), calls=%async_computation.6 | async-start | bytes 3670016 | tf_op jit(solution)/shard_map/all_to_all | solution.py:18
  156.0 3.2 %collective-permute-start.7 = (f32[128,128]{1,0:T(8,128)S(1)}, f32[128,128]{1,0:T(8,128)S(1)}, u32[]{:S(2)}, u32[]{:S(2)}) collective-permute-start(f32[128,128]{1,0:T(8,128)S(1)} %convolution_bitcast_fusion), channel_id=1, source_target_pairs={{0,16},{16,0},{1,17},{17,1},{2,18},{18,2},{3,19},{19,3},{4,20},{20... | collective-permute-start | bytes 196616 | tf_op jit(solution)/shard_map/ppermute | solution.py:27
  181.1 15.4 %all-to-all-start.7 = ((f32[16,14,128]{2,1,0:T(8,128)}), f32[16,14,128]{2,1,0:T(8,128)S(1)}, u32[]{:S(2)}, u32[]{:S(2)}) async-start(f32[16,14,128]{2,1,0:T(8,128)} %reshape.56), calls=%async_computation.7 | async-start | bytes 262144 | tf_op jit(solution)/shard_map/all_to_all | solution.py:18

commit v3 on v1

v3 whole, which is shorter than its diff:
```python
import functools
import math

import jax
import jax.numpy as jnp
from jax import lax
from jax.experimental import pallas as pl
from jax.experimental.pallas import tpu as pltpu
from jax.sharding import Mesh, PartitionSpec as P

HIGH = lax.Precision.HIGHEST
PLANE = ("x", "y")
LINE = ("core", "z")
EVERY = ("x", "y", "core", "z")
PARAMS = pltpu.CompilerParams(vmem_limit_bytes=40 * 1024 * 1024)
LIGHT = pl.CostEstimate(flops=1, bytes_accessed=1, transcendentals=0)


def exchange(value, axes):
    return lax.all_to_all(value, axes, 0, 0, tiled=True)


def spread(block, axes):
    count = lax.axis_size(axes)
    return exchange(jnp.broadcast_to(block[None], (count, *block.shape)), axes)


def other_core(value):
    return lax.ppermute(value, "core", [(0, 1), (1, 0)])


def gather_plane(block):
    return spread(block, PLANE).reshape(-1, block.shape[1])


def scatter_plane(whole):
    chip = whole.reshape(lax.axis_size(PLANE), -1, whole.shape[1])
    return jnp.sum(exchange(chip, PLANE), axis=0)


def to_core(pair):
    return exchange(pair.reshape(-1, *pair.shape[2:]), LINE).reshape(pair.shape)


def in_hbm(*values):
    return [pltpu.with_memory_space_constraint(v, pltpu.HBM) for v in values]


def call(kernel, shapes, memories, scratch=(), light=False, written=False, **options):
    return pl.pallas_call(
        kernel,
        out_shape=shapes,
        in_specs=[pl.BlockSpec(memory_space=m) for m in memories],
        out_specs=jax.tree.map(
            lambda s: pl.BlockSpec(
                memory_space=pl.ANY if s.memory_space == pltpu.HBM and not written else pltpu.VMEM
            ),
            shapes,
        ),
        scratch_shapes=list(scratch),
        compiler_params=PARAMS,
        cost_estimate=LIGHT if light else None,
        **options,
    )


def sorted_blocks(count, value_ref):
    block = value_ref.shape[1] // (2 * count)
    for half in range(2):
        for i in range(count):
            start = (2 * i + half) * block
            place = (half * count + i) * block
            yield value_ref[:, start : start + block], slice(place, place + block)


def write_halves(count, value_ref, low_out, high_out):
    half = low_out.shape[1]
    for value, to in sorted_blocks(count, value_ref):
        if to.stop <= half:
            low_out[:, to] = value.astype(jnp.float32)
        else:
            high_out[:, to.start - half : to.stop - half] = value.astype(jnp.float32)


def give_grad_kernel(count, gate_ref, up_ref, low_out, high_out, buffer, sem):
    core = lax.axis_index("core")
    for which, ref in ((0, up_ref), (1, gate_ref)):

        @pl.when(core == which)
        def _(ref=ref):
            copy = pltpu.make_async_copy(ref, buffer, sem)
            copy.start()
            copy.wait()

    write_halves(count, buffer, low_out, high_out)


def give_act_kernel(count, act_ref, low_out, high_out):
    write_halves(count, act_ref, low_out, high_out)


def give(act, gate, up):
    count = lax.axis_size(PLANE)
    tokens, columns = gate.shape
    grads = [pltpu.VMEM((tokens, columns // 2), jnp.float32)] * 2
    grads = call(
        functools.partial(give_grad_kernel, count),
        grads,
        [pl.ANY] * 2,
        [pltpu.VMEM((tokens, columns), gate.dtype), pltpu.SemaphoreType.DMA],
        light=True,
    )(*in_hbm(gate, up))
    acts = [pltpu.VMEM((tokens, act.shape[1] // 2), jnp.float32)] * 2
    acts = call(functools.partial(give_act_kernel, count), acts, [pltpu.VMEM], light=True)(act)
    return *acts, *grads


def turn(value):
    return value.astype(jnp.float32).T.astype(jnp.bfloat16)


def own_stores(outs, scratch):
    tokens = scratch[0].shape[0]
    staged, sems = scratch[2:6], scratch[6]
    return [
        pltpu.make_async_copy(
            staged[i],
            outs[i].at[:, :tokens] if i % 2 else outs[i].at[:tokens, :],
            sems.at[2 + i],
        )
        for i in range(4)
    ]


def own_part(count, act_ref, grad_ref, outs, scratch):
    staged, sems = scratch[2:6], scratch[6]
    loads = [
        pltpu.make_async_copy(ref, scratch[i], sems.at[i])
        for i, ref in enumerate((act_ref, grad_ref))
    ]
    for load in loads:
        load.start()
    stores = own_stores(outs, scratch)
    for i in range(2):
        rows, turned = staged[2 * i : 2 * i + 2]
        loads[i].wait()
        for value, to in sorted_blocks(count, scratch[i]):
            rows[:, to] = value
        stores[2 * i].start()
        turned[...] = turn(rows[...])
        stores[2 * i + 1].start()


def keep_kernel(count, line_ref, act_ref, gate_ref, lines_out, *refs):
    outs, scratch, line_sem = refs[:4], refs[4:-1], refs[-1]
    copies = [
        pltpu.make_async_copy(line_ref, lines_out.at[i], line_sem.at[i]) for i in range(count)
    ]
    for copy in copies:
        copy.start()

    @pl.when(lax.axis_index("core") == 0)
    def _():
        own_part(count, act_ref, gate_ref, outs, scratch)
        for store in own_stores(outs, scratch):
            store.wait()

    for copy in copies:
        copy.wait()


def merge_kernel(count, act_ref, up_ref, *refs):
    takes, outs, scratch, others = refs[:4], refs[8:12], refs[12:19], refs[19:]
    buffers, staged, (load_sems, store_sems) = others[:4], others[4:8], others[8:]
    loads = [
        pltpu.make_async_copy(take, buffer, load_sems.at[i])
        for i, (take, buffer) in enumerate(zip(takes, buffers))
    ]
    for load in loads:
        load.start()

    @pl.when(lax.axis_index("core") == 1)
    def _():
        own_part(count, act_ref, up_ref, outs, scratch)

    tokens = buffers[0].shape[0]
    stores = []
    for i in range(2):
        rows, turned = staged[2 * i : 2 * i + 2]
        half = buffers[2 * i].shape[1]
        for j in range(2):
            loads[2 * i + j].wait()
            to = slice(j * half, (j + 1) * half)
            value = buffers[2 * i + j][...]
            rows[:, to] = value.astype(jnp.bfloat16)
            turned[to, :] = value.T.astype(jnp.bfloat16)
        stores += [
            pltpu.make_async_copy(rows, outs[2 * i].at[tokens:, :], store_sems.at[2 * i]),
            pltpu.make_async_copy(
                turned, outs[2 * i + 1].at[:, tokens:], store_sems.at[2 * i + 1]
            ),
        ]
        for store in stores[-2:]:
            store.start()
    for store in stores:
        store.wait()

    @pl.when(lax.axis_index("core") == 1)
    def _():
        for store in own_stores(outs, scratch):
            store.wait()


def chip_arrays(act, gate, up, line, taken):
    count = lax.axis_size(PLANE)
    tokens = act.shape[0]
    kinds = [
        (shape, act.dtype)
        for v in (act, gate)
        for shape in ((tokens, v.shape[1]), (v.shape[1], tokens))
    ]
    scratch = [
        pltpu.VMEM(act.shape, act.dtype),
        pltpu.VMEM(gate.shape, gate.dtype),
        *[pltpu.VMEM(*kind) for kind in kinds],
        pltpu.SemaphoreType.DMA((6,)),
    ]
    wholes = [
        pltpu.HBM(tuple(2 * n if n == tokens else n for n in shape), kind)
        for shape, kind in kinds
    ]
    lines, *partly = call(
        functools.partial(keep_kernel, count),
        [pltpu.HBM((count, *line.shape), line.dtype), *wholes],
        [pltpu.VMEM, pl.ANY, pl.ANY],
        [*scratch, pltpu.SemaphoreType.DMA((count,))],
        light=True,
    )(line, *in_hbm(act, gate))

    def finish():
        buffers = [pltpu.VMEM(t.shape, t.dtype) for t in taken]
        sems = [pltpu.SemaphoreType.DMA((4,))] * 2
        return call(
            functools.partial(merge_kernel, count),
            wholes,
            [pl.ANY] * 10,
            [*scratch, *buffers, *scratch[2:6], *sems],
            light=True,
            input_output_aliases={6 + i: i for i in range(4)},
        )(*in_hbm(act, up, *taken), *partly)

    return lines, finish


def halves(value):
    high = value.astype(jnp.bfloat16)
    low = (value - high.astype(jnp.float32)).astype(jnp.bfloat16)
    return jnp.concatenate([high, low], axis=1)


def fold(value):
    columns = value.shape[1] // 2
    return value[:, :columns] + value[:, columns:]


def product(left, right):
    return fold(jnp.dot(left, right, preferred_element_type=jnp.float32))


def joined(low, high):
    lane = lax.broadcasted_iota(jnp.int32, low.shape, 1)
    return jnp.where(lane < low.shape[1] // 2, low, high)


def doubled(value):
    return value + pltpu.roll(value, value.shape[1] // 2, 1)


def small_kernel(grad_ref, state_ref, out_ref, buffer, sems):
    steps = sems.shape[0]
    step = grad_ref.shape[0] // steps
    copies = []
    for i in range(steps):
        at = slice(i * step, (i + 1) * step)
        copies.append(pltpu.make_async_copy(grad_ref.at[at, :], buffer.at[at, :], sems.at[i]))
        copies[-1].start()
    state = halves(state_ref[...])
    columns = state.shape[0]
    for i in range(steps):
        at = slice(i * step, (i + 1) * step)
        copies[i].wait()
        out_ref[at, :] = doubled(
            joined(product(buffer[at, :columns], state), product(buffer[at, columns:], state))
        )


def tall_kernel(turned_ref, factor_ref, out_ref):
    factor = halves(factor_ref[...])
    rows = out_ref.shape[0]
    out_ref[...] = joined(
        product(turned_ref[:rows, :], factor), product(turned_ref[rows:, :], factor)
    )


def tall_product(turned, factor):
    shape = (turned.shape[0] // 2, factor.shape[1])
    return call(tall_kernel, pltpu.VMEM(shape, jnp.float32), [pltpu.VMEM] * 2)(turned, factor)


def streamed_kernel(turned_ref, factor_ref, out_ref, staged, sems):
    factor = halves(factor_ref[...])
    steps = sems.shape[0]
    rows = out_ref.shape[0]
    step = rows // steps
    copies = []
    for i in range(steps):
        at = slice(i * step, (i + 1) * step)
        other = slice(rows + i * step, rows + (i + 1) * step)
        staged[at, :] = joined(
            product(turned_ref[at, :], factor), product(turned_ref[other, :], factor)
        )
        copies.append(pltpu.make_async_copy(staged.at[at, :], out_ref.at[at, :], sems.at[i]))
        copies[-1].start()
    for copy in copies:
        copy.wait()


def streamed_product(turned, factor):
    shape = (turned.shape[0] // 2, factor.shape[1])
    return call(
        streamed_kernel,
        pltpu.HBM(shape, jnp.float32),
        [pltpu.VMEM] * 2,
        [pltpu.VMEM(shape, jnp.float32), pltpu.SemaphoreType.DMA((4,))],
    )(turned, factor)


def project_kernel(factor, rows_ref, raw_ref, out_ref):
    raw = halves(raw_ref[...])
    columns = raw.shape[0]
    out_ref[...] = factor * doubled(
        joined(product(rows_ref[:, :columns], raw), product(rows_ref[:, columns:], raw))
    )


def pack_kernel(after_ref, inverse_ref, rows_ref, out_ref):
    del after_ref
    rank = inverse_ref.shape[0]
    out_ref[:rank, :rank] = inverse_ref[...]
    out_ref[:rank, rank:] = jnp.zeros_like(inverse_ref)
    out_ref[rank:, :] = rows_ref[...]


def pack(after, inverse, rows):
    shape = (inverse.shape[0] + rows.shape[0], rows.shape[1])
    return call(
        pack_kernel, pltpu.VMEM(shape, jnp.float32), [pl.ANY, pltpu.VMEM, pltpu.VMEM], light=True
    )(after, inverse, rows)


def end_kernel(stretch, parts_ref, mine_ref, other_ref, *outs):
    rank = outs[0].shape[1]
    core = lax.axis_index("core")

    def dot(left, right):
        return jnp.dot(left, right, precision=HIGH, preferred_element_type=jnp.float32)

    def write(own):
        for which, ref in enumerate((mine_ref, other_ref) if own == 0 else (other_ref, mine_ref)):
            inverse = ref[:rank, :rank]
            rows = ref[rank:, own * rank : (own + 1) * rank]
            outs[2 * which][...] = dot(rows, inverse) * stretch
            outs[2 * which + 1][...] = dot(jnp.sum(parts_ref[which], axis=0), inverse)

    pl.when(core == 0)(lambda: write(0))
    pl.when(core == 1)(lambda: write(1))


def shards(activations, grad_gate, grad_up, state_gate, state_up):
    devices = lax.axis_size(EVERY)
    tokens, width = activations.shape
    factor = 1.0 / math.sqrt(tokens * devices)
    rows, rank = state_gate.shape
    both = 2 * rank
    line_size = lax.axis_size("z")

    states = jnp.stack([state_gate, state_up])[:, None]
    states = to_core(jnp.broadcast_to(states, (2, line_size, rows, rank)))
    line = jnp.concatenate([states[0], states[1]], axis=-1).reshape(-1, both)

    taken = [other_core(piece) for piece in give(activations, grad_gate, grad_up)]
    lines, finish = chip_arrays(activations, grad_gate, grad_up, line, taken)
    state = exchange(lines, PLANE).reshape(-1, both)
    act, act_turned, grad, grad_turned = finish()

    small = call(
        small_kernel,
        pltpu.VMEM((2 * tokens, both), jnp.float32),
        [pl.ANY, pltpu.VMEM],
        [pltpu.VMEM(grad.shape, grad.dtype), pltpu.SemaphoreType.DMA((2,))],
    )(*in_hbm(grad), state)
    summed = scatter_plane(tall_product(act_turned, small)).reshape(line_size, -1, both)
    mine = jnp.sum(exchange(summed, "z"), axis=0) * jnp.float32(factor)
    raw = gather_plane(spread(mine, "z").reshape(-1, both))

    project = call(
        functools.partial(project_kernel, factor),
        pltpu.VMEM((2 * tokens, both), jnp.float32),
        [pltpu.VMEM] * 2,
    )(act, raw)
    summed = scatter_plane(streamed_product(grad_turned, project)).reshape(line_size, rows, both)
    parts = to_core(jnp.stack([summed[..., :rank], summed[..., rank:]]))

    gram = lax.dot_general(
        raw, raw, (((0,), (0,)), ((), ())), precision=HIGH, preferred_element_type=jnp.float32
    )
    gram = gram[:rank, :rank] + gram[rank:, rank:]
    lower = jnp.linalg.cholesky(gram, symmetrize_input=False)
    inverse = lax.linalg.triangular_solve(
        lower, jnp.eye(rank, dtype=jnp.float32), left_side=False, lower=True, transpose_a=True
    )
    packed = pack(summed, inverse, mine)

    shapes = [pltpu.HBM((n, rank), jnp.float32) for _ in range(2) for n in (mine.shape[0], rows)]
    return tuple(
        call(
            functools.partial(end_kernel, math.sqrt(width)), shapes, [pltpu.VMEM] * 3, written=True
        )(parts, packed, other_core(packed))
    )


def solution(mesh):
    wide, narrow = mesh.devices.shape
    side = math.isqrt(wide // 2)
    fine = Mesh(mesh.devices.reshape(side, side, 2, narrow), EVERY)
    rows = P(EVERY, None)
    return jax.shard_map(
        shards,
        mesh=fine,
        in_specs=(rows,) * 5,
        out_specs=(rows,) * 4,
        check_vma=False,
    )
```

time: 259 us -> 193 us (0.75)
  blocking collectives: 121 us -> 66.8 us
  local copies, waits for them, and re-layouts: 33 us -> 3.59 us
  starting transfers between devices: 28.2 us -> 55.3 us
  other arithmetic: 39.6 us -> 15 us
  Pallas kernels: 0 us -> 21 us
  matrix products: 10.7 us -> 2.04 us
  waiting for transfers between devices: 22.9 us -> 27.3 us
    all_to_all x6 -> x4, blocking collectives: 121 us -> 66.8 us  [exchange(): return lax.all_to_all(value, axes, 0, 0, tiled=True)]
    all_to_all x2 -> x4, starting transfers between devices: 7.93 us -> 40.8 us  [exchange(): return lax.all_to_all(value, axes, 0, 0, tiled=True)]
    pallas_call x0 -> x10, Pallas kernels: none -> 21 us  [the longest x1 8.13 us: finish(): call(functools.partial(merge_kernel, count), wholes, [pl.ANY] * 10, [*scr...]
    all_to_all x2 -> x4, waiting for transfers between devices: 11.4 us -> 24.6 us  [exchange(): return lax.all_to_all(value, axes, 0, 0, tiled=True)]
    another operation x13 -> x7, other arithmetic: 24.9 us -> 12.8 us  [the longest x3 6.52 us: shards(): lower = jnp.linalg.cholesky(gram, symmetrize_input=False)]
    ppermute x4 -> x5, waiting for transfers between devices: 11.5 us -> 2.63 us  [other_core(): return lax.ppermute(value, 'core', [(0, 1), (1, 0)])]
    unnamed x20 -> x16, local copies, waits for them, and re-layouts: 10.8 us -> 2.81 us
    convert_element_type x5 -> x0, other arithmetic: 5.87 us -> none  [parts_of(): return [piece.astype(jnp.bfloat16) for piece in (first, second, third)]]
  transfers between devices with their start and end apart: 6 -> 9, of which waited for: 6 -> 6; matrix products, arithmetic and copies ran while one was open for 10% -> 9% of each run, Pallas kernels for 0% -> 7%
where the time goes in v3:
time: 193 us; the launch traced here: 192 us
  blocking collectives  66.8 us (35%)
  starting transfers between devices  55.3 us (29%)
  waiting for transfers between devices  27.3 us (14%)
  Pallas kernels  21 us (11%)
  other arithmetic  15 us (8%)
  local copies, waits for them, and re-layouts  3.59 us (2%)
  matrix products  2.04 us (1%)
    all_to_all x4, blocking collectives, exchange(): return lax.all_to_all(value, axes, 0, 0, tiled=True)  66.8 us
    all_to_all x4, starting transfers between devices, exchange(): return lax.all_to_all(value, axes, 0, 0, tiled=True)  40.8 us
    all_to_all x4, waiting for transfers between devices, exchange(): return lax.all_to_all(value, axes, 0, 0, tiled=True)  24.6 us
    ppermute x5, starting transfers between devices, other_core(): return lax.ppermute(value, 'core', [(0, 1), (1, 0)])  14.5 us
    pallas_call x1, Pallas kernels, finish(): call(functools.partial(merge_kernel, count), wholes, [pl.ANY] * 10, [*scr...  8.13 us
    another operation x3, other arithmetic, shards(): lower = jnp.linalg.cholesky(gram, symmetrize_input=False)  6.52 us
    another operation x2, other arithmetic, shards(): lax.linalg.triangular_solve(lower, jnp.eye(rank, dtype=jnp.float32), left...  5.55 us
  transfers between devices with their start and end apart: 9, of which 6 were waited for; matrix products, arithmetic and copies ran while one was open for 9% of the time, Pallas kernels for 7%

profile of v3, /device:TPU:1, one launch (start us, length us, event | category | flops | bytes accessed | tf_op | source)
XLA Modules:
  0.0 192.0 jit_solution(6846317030650634767)
XLA Ops:
  1.4 0.8 reshape.67
  2.2 16.8 %all-to-all-start = ((f32[32,1,896]{2,1,0:T(1,128)}), f32[32,1,896]{2,1,0:T(1,128)S(1)}, u32[]{:S(2)}, u32[]{:S(2)}) async-start(f32[32,1,896]{2,1,0:T(1,128)} %reshape.67), calls=%async_computation | async-start | bytes 229376 | tf_op jit(solution)/shard_map/all_to_all | solution.py:20
  18.9 3.6 %shard_map.85 = (f32[128,3584]{1,0:T(8,128)}, f32[128,3584]{1,0:T(8,128)}) custom-call(bf16[128,7168]{1,0:T(8,128)(2,1)} %gate_ref.3, bf16[128,7168]{1,0:T(8,128)(2,1)} %up_ref.3), custom_call_target="tpu_custom_call" | custom-call | flops 1 | bytes 1 | tf_op jit(solution)/shard_map/pallas_call | solution.py:106
  22.6 2.1 %collective-permute-start.2 = (f32[128,3584]{1,0:T(8,128)}, f32[128,3584]{1,0:T(8,128)}, u32[]{:S(2)}, u32[]{:S(2)}) collective-permute-start(f32[128,3584]{1,0:T(8,128)} %get-tuple-element.19), channel_id=1, source_target_pairs={{0,16},{16,0},{1,17},{17,1},{2,18},{18,2},{3,19},{19,3},{4,20},{20... | collective-permute-start | bytes 5505032 | tf_op jit(solution)/shard_map/ppermute | solution.py:29
  24.7 2.2 %collective-permute-start.3 = (f32[128,3584]{1,0:T(8,128)}, f32[128,3584]{1,0:T(8,128)}, u32[]{:S(2)}, u32[]{:S(2)}) collective-permute-start(f32[128,3584]{1,0:T(8,128)} %get-tuple-element.20), channel_id=1, source_target_pairs={{0,16},{16,0},{1,17},{17,1},{2,18},{18,2},{3,19},{19,3},{4,20},{20... | collective-permute-start | bytes 5505032 | tf_op jit(solution)/shard_map/ppermute | solution.py:29
  26.9 7.7 %all-to-all-done = f32[32,1,896]{2,1,0:T(1,128)S(1)} async-done(((f32[32,1,896]{2,1,0:T(1,128)}), f32[32,1,896]{2,1,0:T(1,128)S(1)}, u32[]{:S(2)}, u32[]{:S(2)}) %all-to-all-start) | async-done | bytes 114720 | tf_op jit(solution)/shard_map/all_to_all | solution.py:20
  35.2 0.9 reduce.6
  36.4 1.5 shard_map.86
  37.9 6.9 %all-to-all-start.1 = ((f32[16,224,128]{2,1,0:T(8,128)}), f32[16,224,128]{2,1,0:T(8,128)S(1)}, u32[]{:S(2)}, u32[]{:S(2)}) async-start(f32[16,224,128]{2,1,0:T(8,128)} %get-tuple-element.29), calls=%async_computation.1 | async-start | bytes 3670016 | tf_op jit(solution)/shard_map/all_to_all | solution.py:20
  45.1 6.1 %collective-permute-start = (f32[128,2048]{1,0:T(8,128)S(1)}, f32[128,2048]{1,0:T(8,128)S(1)}, u32[]{:S(2)}, u32[]{:S(2)}) collective-permute-start(f32[128,2048]{1,0:T(8,128)S(1)} %get-tuple-element.17), channel_id=1, source_target_pairs={{0,16},{16,0},{1,17},{17,1},{2,18},{18,2},{3,19},{19,3},{4,20},{20... | collective-permute-start | bytes 3145736 | tf_op jit(solution)/shard_map/ppermute | solution.py:29
  51.2 1.9 %collective-permute-start.1 = (f32[128,2048]{1,0:T(8,128)S(1)}, f32[128,2048]{1,0:T(8,128)S(1)}, u32[]{:S(2)}, u32[]{:S(2)}) collective-permute-start(f32[128,2048]{1,0:T(8,128)S(1)} %get-tuple-element.18), channel_id=1, source_target_pairs={{0,16},{16,0},{1,17},{17,1},{2,18},{18,2},{3,19},{19,3},{4,20},{20... | collective-permute-start | bytes 3145736 | tf_op jit(solution)/shard_map/ppermute | solution.py:29
  53.5 2.3 %collective-permute-done.1.refs_1_ = f32[128,2048]{1,0:T(8,128)S(1)} collective-permute-done((f32[128,2048]{1,0:T(8,128)S(1)}, f32[128,2048]{1,0:T(8,128)S(1)}, u32[]{:S(2)}, u32[]{:S(2)}) %collective-permute-start.1) | collective-permute-done | bytes 1048608 | tf_op jit(solution)/shard_map/ppermute | solution.py:29
  55.8 1.0 copy-done.5
  56.8 8.1 %shard_map.87 = (bf16[256,4096]{1,0:T(8,128)(2,1)}, bf16[4096,256]{1,0:T(8,128)(2,1)}, bf16[256,7168]{1,0:T(8,128)(2,1)}, bf16[7168,256]{1,0:T(8,128)(2,1)}) custom-call(bf16[128,4096]{1,0:T(8,128)(2,1)} %act_ref.5, bf16[128,7168]{1,0:T(8,128)(2,1)} %up_ref.3, ...), custom_call_target="tpu_custom_call", output_to_operand_aliasing={{0}: (6, {}), {1}: (7, {}), {2}: (8, {}), {3}: (9, {})} | custom-call | flops 1 | bytes 1 | tf_op jit(solution)/shard_map/pallas_call | solution.py:243
  64.9 0.9 all-to-all-done.1
  65.9 3.1 %shard_map.88.factor_ref = f32[256,128]{1,0:T(8,128)S(1)} custom-call(bf16[256,7168]{1,0:T(8,128)(2,1)} %get-tuple-element.28.grad_ref, f32[3584,128]{1,0:T(8,128)S(1)} %bitcast.25), custom_call_target="tpu_custom_call" | custom-call | tf_op jit(solution)/shard_map/pallas_call | solution.py:396
  69.7 20.5 %all_to_all.40 = f32[16,128,128]{2,1,0:T(8,128)S(1)} all-to-all(f32[16,128,128]{2,1,0:T(8,128)S(1)} %bitcast.26), channel_id=1, replica_groups=mesh['x'=4,'y'=4,'core'=2,'z'=16] {'x','y'}, dimensions={0} | all-to-all | bytes 2097152 | tf_op jit(solution)/shard_map/all_to_all | solution.py:20
  90.3 16.9 %all_to_all.41 = f32[16,8,128]{2,1,0:T(8,128)S(1)} all-to-all(f32[16,8,128]{2,1,0:T(8,128)S(1)} %bitcast.31), channel_id=1, replica_groups=mesh['x'=4,'y'=4,'core'=2,'z'=16] {'z'}, dimensions={0} | all-to-all | bytes 131072 | tf_op jit(solution)/shard_map/all_to_all | solution.py:20
  107.2 14.4 %all_to_all.42 = f32[16,8,128]{2,1,0:T(8,128)S(1)} all-to-all(f32[16,8,128]{2,1,0:T(8,128)S(1)} %broadcast_in_dim.10), channel_id=1, replica_groups=mesh['x'=4,'y'=4,'core'=2,'z'=16] {'z'}, dimensions={0} | all-to-all | bytes 131072 | tf_op jit(solution)/shard_map/all_to_all | solution.py:20
  121.7 15.1 %all_to_all.43 = f32[16,128,128]{2,1,0:T(8,128)S(1)} all-to-all(f32[16,128,128]{2,1,0:T(8,128)S(1)} %broadcast_in_dim.24), channel_id=1, replica_groups=mesh['x'=4,'y'=4,'core'=2,'z'=16] {'x','y'}, dimensions={0} | all-to-all | bytes 2097152 | tf_op jit(solution)/shard_map/all_to_all | solution.py:20
  137.5 1.9 %shard_map.91 = f32[3584,128]{1,0:T(8,128)} custom-call(bf16[7168,256]{1,0:T(8,128)(2,1)S(1)} %copy-done, f32[256,128]{1,0:T(8,128)S(1)} %shard_map.90.factor_ref), custom_call_target="tpu_custom_call" | custom-call | tf_op jit(solution)/shard_map/pallas_call | solution.py:330
  139.5 3.7 %all-to-all-start.6 = ((f32[16,224,128]{2,1,0:T(8,128)}), f32[16,224,128]{2,1,0:T(8,128)S(1)}, u32[]{:S(2)}, u32[]{:S(2)}) async-start(f32[16,224,128]{2,1,0:T(8,128)} %bitcast.28), calls=%async_computation.6 | async-start | bytes 3670016 | tf_op jit(solution)/shard_map/all_to_all | solution.py:20
  143.2 1.9 convolution_bitcast_fusion
  145.2 5.9 %cholesky.14 = f32[64,64]{1,0:T(8,128)S(1)} custom-call(f32[64,64]{1,0:T(8,128)S(1)} %slice_add_fusion), custom_call_target="Cholesky" | custom-call | tf_op jit(solution)/shard_map/jit(cholesky)/cholesky | solution.py:418
  151.7 8.3 %all-to-all-done.6 = f32[16,224,128]{2,1,0:T(8,128)S(1)} async-done(((f32[16,224,128]{2,1,0:T(8,128)}), f32[16,224,128]{2,1,0:T(8,128)S(1)}, u32[]{:S(2)}, u32[]{:S(2)}) %all-to-all-start.6) | async-done | bytes 1835040 | tf_op jit(solution)/shard_map/all_to_all | solution.py:20
  160.2 0.8 reshape.69
  161.0 13.4 %all-to-all-start.7 = ((f32[32,1,896]{2,1,0:T(1,128)}), f32[32,1,896]{2,1,0:T(1,128)S(1)}, u32[]{:S(2)}, u32[]{:S(2)}) async-start(f32[32,1,896]{2,1,0:T(1,128)} %reshape.69), calls=%async_computation.7 | async-start | bytes 229376 | tf_op jit(solution)/shard_map/all_to_all | solution.py:20
  175.1 4.9 %custom-call.6 = f32[1,64,64]{1,2,0:T(8,128)S(1)} custom-call(f32[1,64,64]{2,1,0:T(8,128)S(1)} %fusion), custom_call_target="InvertDiagBlocksLowerTriangular" | custom-call | tf_op jit(solution)/shard_map/triangular_solve | solution.py:419
  180.2 2.2 %collective-permute-start.4 = (f32[72,128]{1,0:T(8,128)S(1)}, f32[72,128]{1,0:T(8,128)S(1)}, u32[]{:S(2)}, u32[]{:S(2)}) collective-permute-start(f32[72,128]{1,0:T(8,128)S(1)} %shard_map.92.mine_ref), channel_id=1, source_target_pairs={{0,16},{16,0},{1,17},{17,1},{2,18},{18,2},{3,19},{19,3},{4,20},{20... | collective-permute-start | bytes 110600 | tf_op jit(solution)/shard_map/ppermute | solution.py:29
  182.3 7.7 %all-to-all-done.7 = f32[32,1,896]{2,1,0:T(1,128)S(1)} async-done(((f32[32,1,896]{2,1,0:T(1,128)}), f32[32,1,896]{2,1,0:T(1,128)S(1)}, u32[]{:S(2)}, u32[]{:S(2)}) %all-to-all-start.7) | async-done | bytes 114720 | tf_op jit(solution)/shard_map/all_to_all | solution.py:20
  190.0 0.9 reduce.7
  191.1 0.9 shard_map.93
  (42 shorter events, 5.7 us)
Async XLA Ops:
  2.2 32.5 %all-to-all-start = ((f32[32,1,896]{2,1,0:T(1,128)}), f32[32,1,896]{2,1,0:T(1,128)S(1)}, u32[]{:S(2)}, u32[]{:S(2)}) async-start(f32[32,1,896]{2,1,0:T(1,128)} %reshape.67), calls=%async_computation | async-start | bytes 229376 | tf_op jit(solution)/shard_map/all_to_all | solution.py:20
  22.6 33.2 %collective-permute-start.2 = (f32[128,3584]{1,0:T(8,128)}, f32[128,3584]{1,0:T(8,128)}, u32[]{:S(2)}, u32[]{:S(2)}) collective-permute-start(f32[128,3584]{1,0:T(8,128)} %get-tuple-element.19), channel_id=1, source_target_pairs={{0,16},{16,0},{1,17},{17,1},{2,18},{18,2},{3,19},{19,3},{4,20},{20... | collective-permute-start | bytes 5505032 | tf_op jit(solution)/shard_map/ppermute | solution.py:29
  24.7 31.0 %collective-permute-start.3 = (f32[128,3584]{1,0:T(8,128)}, f32[128,3584]{1,0:T(8,128)}, u32[]{:S(2)}, u32[]{:S(2)}) collective-permute-start(f32[128,3584]{1,0:T(8,128)} %get-tuple-element.20), channel_id=1, source_target_pairs={{0,16},{16,0},{1,17},{17,1},{2,18},{18,2},{3,19},{19,3},{4,20},{20... | collective-permute-start | bytes 5505032 | tf_op jit(solution)/shard_map/ppermute | solution.py:29
  37.9 6.9 %copy-start.1 = (bf16[128,4096]{1,0:T(8,128)(2,1)S(1)}, bf16[128,4096]{1,0:T(8,128)(2,1)}, u32[]{:S(2)}) copy-start(bf16[128,4096]{1,0:T(8,128)(2,1)} %act_ref.5) | copy-start | bytes 3145732
  37.9 27.9 %all-to-all-start.1 = ((f32[16,224,128]{2,1,0:T(8,128)}), f32[16,224,128]{2,1,0:T(8,128)S(1)}, u32[]{:S(2)}, u32[]{:S(2)}) async-start(f32[16,224,128]{2,1,0:T(8,128)} %get-tuple-element.29), calls=%async_computation.1 | async-start | bytes 3670016 | tf_op jit(solution)/shard_map/all_to_all | solution.py:20
  45.1 8.4 %collective-permute-start = (f32[128,2048]{1,0:T(8,128)S(1)}, f32[128,2048]{1,0:T(8,128)S(1)}, u32[]{:S(2)}, u32[]{:S(2)}) collective-permute-start(f32[128,2048]{1,0:T(8,128)S(1)} %get-tuple-element.17), channel_id=1, source_target_pairs={{0,16},{16,0},{1,17},{17,1},{2,18},{18,2},{3,19},{19,3},{4,20},{20... | collective-permute-start | bytes 3145736 | tf_op jit(solution)/shard_map/ppermute | solution.py:29
  51.2 4.6 %collective-permute-start.1 = (f32[128,2048]{1,0:T(8,128)S(1)}, f32[128,2048]{1,0:T(8,128)S(1)}, u32[]{:S(2)}, u32[]{:S(2)}) collective-permute-start(f32[128,2048]{1,0:T(8,128)S(1)} %get-tuple-element.18), channel_id=1, source_target_pairs={{0,16},{16,0},{1,17},{17,1},{2,18},{18,2},{3,19},{19,3},{4,20},{20... | collective-permute-start | bytes 3145736 | tf_op jit(solution)/shard_map/ppermute | solution.py:29
  53.5 2.3 %copy-start.4 = (f32[128,2048]{1,0:T(8,128)}, f32[128,2048]{1,0:T(8,128)S(1)}, u32[]{:S(2)}) copy-start(f32[128,2048]{1,0:T(8,128)S(1)} %collective-permute-done.refs_0_) | copy-start | bytes 3145732
  55.8 1.0 copy-start.5
  65.9 3.1 %copy-start.3 = (bf16[4096,256]{1,0:T(8,128)(2,1)S(1)}, bf16[4096,256]{1,0:T(8,128)(2,1)}, u32[]{:S(2)}) copy-start(bf16[4096,256]{1,0:T(8,128)(2,1)} %get-tuple-element.27.turned_ref) | copy-start | bytes 6291460
  90.3 46.5 %copy-start.2 = (bf16[256,4096]{1,0:T(8,128)(2,1)S(1)}, bf16[256,4096]{1,0:T(8,128)(2,1)}, u32[]{:S(2)}) copy-start(bf16[256,4096]{1,0:T(8,128)(2,1)} %get-tuple-element.26.rows_ref) | copy-start | bytes 6291460
  121.7 15.9 %copy-start = (bf16[7168,256]{1,0:T(8,128)(2,1)S(1)}, bf16[7168,256]{1,0:T(8,128)(2,1)}, u32[]{:S(2)}) copy-start(bf16[7168,256]{1,0:T(8,128)(2,1)} %get-tuple-element.25.turned_ref) | copy-start | bytes 11010052
  139.5 20.5 %all-to-all-start.6 = ((f32[16,224,128]{2,1,0:T(8,128)}), f32[16,224,128]{2,1,0:T(8,128)S(1)}, u32[]{:S(2)}, u32[]{:S(2)}) async-start(f32[16,224,128]{2,1,0:T(8,128)} %bitcast.28), calls=%async_computation.6 | async-start | bytes 3670016 | tf_op jit(solution)/shard_map/all_to_all | solution.py:20
  161.0 29.0 %all-to-all-start.7 = ((f32[32,1,896]{2,1,0:T(1,128)}), f32[32,1,896]{2,1,0:T(1,128)S(1)}, u32[]{:S(2)}, u32[]{:S(2)}) async-start(f32[32,1,896]{2,1,0:T(1,128)} %reshape.69), calls=%async_computation.7 | async-start | bytes 229376 | tf_op jit(solution)/shard_map/all_to_all | solution.py:20
  180.2 10.9 %collective-permute-start.4 = (f32[72,128]{1,0:T(8,128)S(1)}, f32[72,128]{1,0:T(8,128)S(1)}, u32[]{:S(2)}, u32[]{:S(2)}) collective-permute-start(f32[72,128]{1,0:T(8,128)S(1)} %shard_map.92.mine_ref), channel_id=1, source_target_pairs={{0,16},{16,0},{1,17},{17,1},{2,18},{18,2},{3,19},{19,3},{4,20},{20... | collective-permute-start | bytes 110600 | tf_op jit(solution)/shard_map/ppermute | solution.py:29

commit v4 on v3

--- a/solution.py
+++ b/solution.py
@@ -36,10 +36,6 @@
 def scatter_plane(whole):
     chip = whole.reshape(lax.axis_size(PLANE), -1, whole.shape[1])
     return jnp.sum(exchange(chip, PLANE), axis=0)
-
-
-def to_core(pair):
-    return exchange(pair.reshape(-1, *pair.shape[2:]), LINE).reshape(pair.shape)
 
 
 def in_hbm(*values):
@@ -64,6 +60,64 @@
     )
 
 
+def state_kernel(gate_ref, up_ref, out_ref):
+    half = gate_ref.shape[0] // 2
+    size = out_ref.shape[0] // 2
+    for which, ref in enumerate((gate_ref, up_ref)):
+        message = jnp.concatenate([ref[:half, :], ref[half:, :]], axis=1)
+        for z in range(size):
+            out_ref[which * size + z] = message
+
+
+def state_messages(gate, up):
+    rows, rank = gate.shape
+    shape = (2 * lax.axis_size("z"), rows // 2, 2 * rank)
+    return call(state_kernel, pltpu.VMEM(shape, gate.dtype), [pltpu.VMEM] * 2)(
+        *in_hbm(gate, up)
+    )
+
+
+def write_line(got_ref, line_ref):
+    size, half = got_ref.shape[0] // 2, got_ref.shape[1]
+    rank = got_ref.shape[2] // 2
+    for z in range(size):
+        for part in range(2):
+            columns = slice(part * rank, (part + 1) * rank)
+            start = (2 * z + part) * half
+            line_ref[start : start + half, :] = jnp.concatenate(
+                [got_ref[z, :, columns], got_ref[size + z, :, columns]], axis=1
+            )
+
+
+def sum_kernel(parts_ref, after_ref, out_ref, line_ref):
+    del after_ref
+    line_ref[...] = jnp.sum(parts_ref[...], axis=0)
+    size, half = out_ref.shape[0] // 2, out_ref.shape[1]
+    rank = out_ref.shape[2] // 2
+    for which in range(2):
+        columns = slice(which * rank, (which + 1) * rank)
+        for z in range(size):
+            start = 2 * z * half
+            out_ref[which * size + z] = jnp.concatenate(
+                [
+                    line_ref[start : start + half, columns],
+                    line_ref[start + half : start + 2 * half, columns],
+                ],
+                axis=1,
+            )
+
+
+def sum_messages(parts, after):
+    _, rows, columns = parts.shape
+    size = lax.axis_size("z")
+    return call(
+        sum_kernel,
+        pltpu.VMEM((2 * size, rows // (2 * size), columns), parts.dtype),
+        [pltpu.VMEM, pl.ANY],
+        [pltpu.VMEM((rows, columns), parts.dtype)],
+    )(parts, after)
+
+
 def sorted_blocks(count, value_ref):
     block = value_ref.shape[1] // (2 * count)
     for half in range(2):
@@ -95,24 +149,16 @@
     write_halves(count, buffer, low_out, high_out)
 
 
-def give_act_kernel(count, act_ref, low_out, high_out):
-    write_halves(count, act_ref, low_out, high_out)
-
-
-def give(act, gate, up):
+def give_grad(gate, up):
     count = lax.axis_size(PLANE)
     tokens, columns = gate.shape
-    grads = [pltpu.VMEM((tokens, columns // 2), jnp.float32)] * 2
-    grads = call(
+    return call(
         functools.partial(give_grad_kernel, count),
-        grads,
+        [pltpu.VMEM((tokens, columns // 2), jnp.float32)] * 2,
         [pl.ANY] * 2,
         [pltpu.VMEM((tokens, columns), gate.dtype), pltpu.SemaphoreType.DMA],
         light=True,
     )(*in_hbm(gate, up))
-    acts = [pltpu.VMEM((tokens, act.shape[1] // 2), jnp.float32)] * 2
-    acts = call(functools.partial(give_act_kernel, count), acts, [pltpu.VMEM], light=True)(act)
-    return *acts, *grads
 
 
 def turn(value):
@@ -151,8 +197,9 @@
         stores[2 * i + 1].start()
 
 
-def keep_kernel(count, line_ref, act_ref, gate_ref, lines_out, *refs):
-    outs, scratch, line_sem = refs[:4], refs[4:-1], refs[-1]
+def keep_kernel(count, got_ref, act_ref, gate_ref, lines_out, *refs):
+    outs, scratch, (line_ref, line_sem) = refs[:4], refs[4:-2], refs[-2:]
+    write_line(got_ref, line_ref)
     copies = [
         pltpu.make_async_copy(line_ref, lines_out.at[i], line_sem.at[i]) for i in range(count)
     ]
@@ -169,23 +216,40 @@
         copy.wait()
 
 
-def merge_kernel(count, act_ref, up_ref, *refs):
-    takes, outs, scratch, others = refs[:4], refs[8:12], refs[12:19], refs[19:]
-    buffers, staged, (load_sems, store_sems) = others[:4], others[4:8], others[8:]
+def keep_late_kernel(count, act_ref, up_ref, *refs):
+    outs, (low_out, high_out), scratch = refs[4:8], refs[8:10], refs[10:]
+    late = lax.axis_index("core") == 1
+
+    @pl.when(late)
+    def _():
+        own_part(count, act_ref, up_ref, outs, scratch)
+
+    @pl.when(jnp.logical_not(late))
+    def _():
+        load = pltpu.make_async_copy(act_ref, scratch[0], scratch[6].at[0])
+        load.start()
+        load.wait()
+
+    write_halves(count, scratch[0], low_out, high_out)
+
+    @pl.when(late)
+    def _():
+        for store in own_stores(outs, scratch):
+            store.wait()
+
+
+def merge_kernel(*refs):
+    takes, outs = refs[:4], refs[8:12]
+    buffers, staged, (load_sems, store_sems) = refs[12:16], refs[16:20], refs[20:]
     loads = [
         pltpu.make_async_copy(take, buffer, load_sems.at[i])
         for i, (take, buffer) in enumerate(zip(takes, buffers))
     ]
     for load in loads:
         load.start()
-
-    @pl.when(lax.axis_index("core") == 1)
-    def _():
-        own_part(count, act_ref, up_ref, outs, scratch)
-
     tokens = buffers[0].shape[0]
     stores = []
-    for i in range(2):
+    for i in (1, 0):
         rows, turned = staged[2 * i : 2 * i + 2]
         half = buffers[2 * i].shape[1]
         for j in range(2):
@@ -205,13 +269,8 @@
     for store in stores:
         store.wait()
 
-    @pl.when(lax.axis_index("core") == 1)
-    def _():
-        for store in own_stores(outs, scratch):
-            store.wait()
-
-
-def chip_arrays(act, gate, up, line, taken):
+
+def chip_arrays(act, gate, up, got):
     count = lax.axis_size(PLANE)
     tokens = act.shape[0]
     kinds = [
@@ -229,27 +288,39 @@
         pltpu.HBM(tuple(2 * n if n == tokens else n for n in shape), kind)
         for shape, kind in kinds
     ]
+    line = got.shape[0] * got.shape[1], got.shape[2]
     lines, *partly = call(
         functools.partial(keep_kernel, count),
-        [pltpu.HBM((count, *line.shape), line.dtype), *wholes],
+        [pltpu.HBM((count, *line), got.dtype), *wholes],
         [pltpu.VMEM, pl.ANY, pl.ANY],
-        [*scratch, pltpu.SemaphoreType.DMA((count,))],
+        [*scratch, pltpu.VMEM(line, got.dtype), pltpu.SemaphoreType.DMA((count,))],
         light=True,
-    )(line, *in_hbm(act, gate))
-
-    def finish():
-        buffers = [pltpu.VMEM(t.shape, t.dtype) for t in taken]
-        sems = [pltpu.SemaphoreType.DMA((4,))] * 2
-        return call(
-            functools.partial(merge_kernel, count),
-            wholes,
-            [pl.ANY] * 10,
-            [*scratch, *buffers, *scratch[2:6], *sems],
-            light=True,
-            input_output_aliases={6 + i: i for i in range(4)},
-        )(*in_hbm(act, up, *taken), *partly)
-
-    return lines, finish
+    )(got, *in_hbm(act, gate))
+
+    half = pltpu.VMEM((tokens, act.shape[1] // 2), jnp.float32)
+    *partly, low, high = call(
+        functools.partial(keep_late_kernel, count),
+        [*wholes, half, half],
+        [pl.ANY] * 6,
+        scratch,
+        light=True,
+        input_output_aliases={2 + i: i for i in range(4)},
+    )(*in_hbm(act, up), *partly)
+
+    grads = [other_core(piece) for piece in give_grad(gate, up)]
+    taken = [other_core(low), other_core(high), *grads]
+    return lines, call(
+        merge_kernel,
+        wholes,
+        [pl.ANY] * 8,
+        [
+            *[pltpu.VMEM(t.shape, t.dtype) for t in taken],
+            *scratch[2:6],
+            *[pltpu.SemaphoreType.DMA((4,))] * 2,
+        ],
+        light=True,
+        input_output_aliases={4 + i: i for i in range(4)},
+    )(*taken, *partly)
 
 
 def halves(value):
@@ -370,7 +441,10 @@
             inverse = ref[:rank, :rank]
             rows = ref[rank:, own * rank : (own + 1) * rank]
             outs[2 * which][...] = dot(rows, inverse) * stretch
-            outs[2 * which + 1][...] = dot(jnp.sum(parts_ref[which], axis=0), inverse)
+            size = parts_ref.shape[0] // 2
+            message = jnp.sum(parts_ref[which * size : (which + 1) * size], axis=0)
+            summed = jnp.concatenate([message[:, :rank], message[:, rank:]], axis=0)
+            outs[2 * which + 1][...] = dot(summed, inverse)
 
     pl.when(core == 0)(lambda: write(0))
     pl.when(core == 1)(lambda: write(1))
@@ -384,14 +458,11 @@
     both = 2 * rank
     line_size = lax.axis_size("z")
 
-    states = jnp.stack([state_gate, state_up])[:, None]
-    states = to_core(jnp.broadcast_to(states, (2, line_size, rows, rank)))
-    line = jnp.concatenate([states[0], states[1]], axis=-1).reshape(-1, both)
-
-    taken = [other_core(piece) for piece in give(activations, grad_gate, grad_up)]
-    lines, finish = chip_arrays(activations, grad_gate, grad_up, line, taken)
+    got = exchange(state_messages(state_gate, state_up), LINE)
+    lines, (act, act_turned, grad, grad_turned) = chip_arrays(
+        activations, grad_gate, grad_up, got
+    )
     state = exchange(lines, PLANE).reshape(-1, both)
-    act, act_turned, grad, grad_turned = finish()
 
     small = call(
         small_kernel,
@@ -408,9 +479,6 @@
         pltpu.VMEM((2 * tokens, both), jnp.float32),
         [pltpu.VMEM] * 2,
     )(act, raw)
-    summed = scatter_plane(streamed_product(grad_turned, project)).reshape(line_size, rows, both)
-    parts = to_core(jnp.stack([summed[..., :rank], summed[..., rank:]]))
-
     gram = lax.dot_general(
         raw, raw, (((0,), (0,)), ((), ())), precision=HIGH, preferred_element_type=jnp.float32
     )
@@ -419,7 +487,12 @@
     inverse = lax.linalg.triangular_solve(
         lower, jnp.eye(rank, dtype=jnp.float32), left_side=False, lower=True, transpose_a=True
     )
-    packed = pack(summed, inverse, mine)
+
+    partial = streamed_product(grad_turned, project)
+    received = exchange(partial.reshape(lax.axis_size(PLANE), -1, both), PLANE)
+    messages = sum_messages(received, inverse)
+    parts = exchange(messages, LINE)
+    packed = pack(messages, inverse, mine)
 
     shapes = [pltpu.HBM((n, rank), jnp.float32) for _ in range(2) for n in (mine.shape[0], rows)]
     return tuple(

time: 193 us -> 190 us (0.984)
  waiting for transfers between devices: 27.3 us -> 31.2 us
  Pallas kernels: 21 us -> 24.5 us
  local copies, waits for them, and re-layouts: 3.59 us -> 0.11 us
  other arithmetic: 15 us -> 12.2 us
  starting transfers between devices: 55.3 us -> 52.7 us
    pallas_call x4 -> x6, Pallas kernels: 13.5 us -> 17.1 us  [the longest x1 5.07 us: chip_arrays(): call(merge_kernel, wholes, [pl.ANY] * 8, [*[pltpu.VMEM(t.shape, t.dtype)...]
    all_to_all x4, waiting for transfers between devices: 24.6 us -> 27.6 us  [exchange(): return lax.all_to_all(value, axes, 0, 0, tiled=True)]
    unnamed x16 -> x6, local copies, waits for them, and re-layouts: 2.81 us -> 0.01 us
    ppermute x5, starting transfers between devices: 14.5 us -> 11.8 us  [other_core(): return lax.ppermute(value, 'core', [(0, 1), (1, 0)])]
  transfers between devices with their start and end apart: 9 -> 9, of which waited for: 6 -> 7; matrix products, arithmetic and copies ran while one was open for 9% -> 7% of each run, Pallas kernels for 7% -> 8%
where the time goes in v4:
time: 190 us
  blocking collectives  66.1 us (35%)
  starting transfers between devices  52.7 us (28%)
  waiting for transfers between devices  31.2 us (16%)
  Pallas kernels  24.5 us (13%)
  other arithmetic  12.2 us (6%)
  matrix products  2.03 us (1%)
    all_to_all x4, blocking collectives, exchange(): return lax.all_to_all(value, axes, 0, 0, tiled=True)  66.1 us
    all_to_all x4, starting transfers between devices, exchange(): return lax.all_to_all(value, axes, 0, 0, tiled=True)  40.8 us
    all_to_all x4, waiting for transfers between devices, exchange(): return lax.all_to_all(value, axes, 0, 0, tiled=True)  27.6 us
    ppermute x5, starting transfers between devices, other_core(): return lax.ppermute(value, 'core', [(0, 1), (1, 0)])  11.8 us
    another operation x3, other arithmetic, shards(): lower = jnp.linalg.cholesky(gram, symmetrize_input=False)  6.52 us
    another operation x2, other arithmetic, shards(): lax.linalg.triangular_solve(lower, jnp.eye(rank, dtype=jnp.float32), left...  5.55 us
    pallas_call x1, Pallas kernels, chip_arrays(): call(merge_kernel, wholes, [pl.ANY] * 8, [*[pltpu.VMEM(t.shape, t.dtype)...  5.07 us
    pallas_call x1, Pallas kernels, chip_arrays(): call(functools.partial(keep_late_kernel, count), [*wholes, half, half], [...  4.5 us
  transfers between devices with their start and end apart: 9, of which 7 were waited for; matrix products, arithmetic and copies ran while one was open for 7% of the time, Pallas kernels for 8%

profile of v4, /device:TPU:1, one launch (start us, length us, event | category | flops | bytes accessed | tf_op | source)
XLA Modules:
  0.0 189.7 jit_solution(836805897790747466)
XLA Ops:
  0.6 1.4 shard_map.84
  2.1 16.8 %all-to-all-start = ((f32[32,7,128]{2,1,0:T(8,128)}), f32[32,7,128]{2,1,0:T(8,128)S(1)}, u32[]{:S(2)}, u32[]{:S(2)}) async-start(f32[32,7,128]{2,1,0:T(8,128)} %shard_map.84), calls=%async_computation | async-start | bytes 262144 | tf_op jit(solution)/shard_map/all_to_all | solution.py:20
  18.8 3.6 %shard_map.87 = (f32[128,3584]{1,0:T(8,128)}, f32[128,3584]{1,0:T(8,128)}) custom-call(bf16[128,7168]{1,0:T(8,128)(2,1)} %gate_ref.5, bf16[128,7168]{1,0:T(8,128)(2,1)} %up_ref.5), custom_call_target="tpu_custom_call" | custom-call | flops 1 | bytes 1 | tf_op jit(solution)/shard_map/pallas_call | solution.py:155
  22.5 2.1 %collective-permute-start.2 = (f32[128,3584]{1,0:T(8,128)}, f32[128,3584]{1,0:T(8,128)}, u32[]{:S(2)}, u32[]{:S(2)}) collective-permute-start(f32[128,3584]{1,0:T(8,128)} %get-tuple-element.27), channel_id=1, source_target_pairs={{0,16},{16,0},{1,17},{17,1},{2,18},{18,2},{3,19},{19,3},{4,20},{20... | collective-permute-start | bytes 5505032 | tf_op jit(solution)/shard_map/ppermute | solution.py:29
  24.6 2.2 %collective-permute-start.3 = (f32[128,3584]{1,0:T(8,128)}, f32[128,3584]{1,0:T(8,128)}, u32[]{:S(2)}, u32[]{:S(2)}) collective-permute-start(f32[128,3584]{1,0:T(8,128)} %get-tuple-element.28), channel_id=1, source_target_pairs={{0,16},{16,0},{1,17},{17,1},{2,18},{18,2},{3,19},{19,3},{4,20},{20... | collective-permute-start | bytes 5505032 | tf_op jit(solution)/shard_map/ppermute | solution.py:29
  26.8 8.4 %all-to-all-done.got_ref = f32[32,7,128]{2,1,0:T(8,128)S(1)} async-done(((f32[32,7,128]{2,1,0:T(8,128)}), f32[32,7,128]{2,1,0:T(8,128)S(1)}, u32[]{:S(2)}, u32[]{:S(2)}) %all-to-all-start) | async-done | bytes 114720 | tf_op jit(solution)/shard_map/all_to_all | solution.py:20
  35.2 1.5 shard_map.85
  36.7 6.8 %all-to-all-start.1 = ((f32[16,224,128]{2,1,0:T(8,128)}), f32[16,224,128]{2,1,0:T(8,128)S(1)}, u32[]{:S(2)}, u32[]{:S(2)}) async-start(f32[16,224,128]{2,1,0:T(8,128)} %get-tuple-element.37), calls=%async_computation.1 | async-start | bytes 3670016 | tf_op jit(solution)/shard_map/all_to_all | solution.py:20
  43.5 4.5 %shard_map.86 = (bf16[256,4096]{1,0:T(8,128)(2,1)}, bf16[4096,256]{1,0:T(8,128)(2,1)}, bf16[256,7168]{1,0:T(8,128)(2,1)}, bf16[7168,256]{1,0:T(8,128)(2,1)}, f32...) custom-call(bf16[128,4096]{1,0:T(8,128)(2,1)} %act_ref.3, ...), custom_call_target="tpu_custom_call", output_to_operand_aliasing={{0}: (2, {}), {1}: (3, {}), {2}: (4, {}), {3}: (5, {})} | custom-call | flops 1 | bytes 1 | tf_op jit(solution)/shard_map/pallas_call | solution.py:301
  48.0 3.4 %collective-permute-start = (f32[128,2048]{1,0:T(8,128)S(1)}, f32[128,2048]{1,0:T(8,128)S(1)}, u32[]{:S(2)}, u32[]{:S(2)}) collective-permute-start(f32[128,2048]{1,0:T(8,128)S(1)} %get-tuple-element.25), channel_id=1, source_target_pairs={{0,16},{16,0},{1,17},{17,1},{2,18},{18,2},{3,19},{19,3},{4,20},{20... | collective-permute-start | bytes 3145736 | tf_op jit(solution)/shard_map/ppermute | solution.py:29
  51.5 1.9 %collective-permute-start.1 = (f32[128,2048]{1,0:T(8,128)S(1)}, f32[128,2048]{1,0:T(8,128)S(1)}, u32[]{:S(2)}, u32[]{:S(2)}) collective-permute-start(f32[128,2048]{1,0:T(8,128)S(1)} %get-tuple-element.26), channel_id=1, source_target_pairs={{0,16},{16,0},{1,17},{17,1},{2,18},{18,2},{3,19},{19,3},{4,20},{20... | collective-permute-start | bytes 3145736 | tf_op jit(solution)/shard_map/ppermute | solution.py:29
  53.7 2.3 %collective-permute-done.1.refs_1_ = f32[128,2048]{1,0:T(8,128)S(1)} collective-permute-done((f32[128,2048]{1,0:T(8,128)S(1)}, f32[128,2048]{1,0:T(8,128)S(1)}, u32[]{:S(2)}, u32[]{:S(2)}) %collective-permute-start.1) | collective-permute-done | bytes 1048608 | tf_op jit(solution)/shard_map/ppermute | solution.py:29
  56.0 5.1 %shard_map.88 = (bf16[256,4096]{1,0:T(8,128)(2,1)}, bf16[4096,256]{1,0:T(8,128)(2,1)}, bf16[256,7168]{1,0:T(8,128)(2,1)}, bf16[7168,256]{1,0:T(8,128)(2,1)}) custom-call(f32[128,2048]{1,0:T(8,128)S(1)} %collective-permute-done.refs_0_, ...), custom_call_target="tpu_custom_call", output_to_operand_aliasing={{0}: (4, {}), {1}: (5, {}), {2}: (6, {}), {3}: (7, {})} | custom-call | flops 1 | bytes 1 | tf_op jit(solution)/shard_map/pallas_call | solution.py:312
  61.1 3.6 %all-to-all-done.1 = f32[16,224,128]{2,1,0:T(8,128)S(1)} async-done(((f32[16,224,128]{2,1,0:T(8,128)}), f32[16,224,128]{2,1,0:T(8,128)S(1)}, u32[]{:S(2)}, u32[]{:S(2)}) %all-to-all-start.1) | async-done | bytes 1835040 | tf_op jit(solution)/shard_map/all_to_all | solution.py:20
  64.7 3.1 %shard_map.89.factor_ref = f32[256,128]{1,0:T(8,128)S(1)} custom-call(bf16[256,7168]{1,0:T(8,128)(2,1)} %get-tuple-element.36.grad_ref, f32[3584,128]{1,0:T(8,128)S(1)} %bitcast.16), custom_call_target="tpu_custom_call" | custom-call | tf_op jit(solution)/shard_map/pallas_call | solution.py:467
  68.6 22.0 %all_to_all.40 = f32[16,128,128]{2,1,0:T(8,128)S(1)} all-to-all(f32[16,128,128]{2,1,0:T(8,128)S(1)} %bitcast.17), channel_id=1, replica_groups=mesh['x'=4,'y'=4,'core'=2,'z'=16] {'x','y'}, dimensions={0} | all-to-all | bytes 2097152 | tf_op jit(solution)/shard_map/all_to_all | solution.py:20
  90.6 14.6 %all_to_all.41 = f32[16,8,128]{2,1,0:T(8,128)S(1)} all-to-all(f32[16,8,128]{2,1,0:T(8,128)S(1)} %bitcast.19), channel_id=1, replica_groups=mesh['x'=4,'y'=4,'core'=2,'z'=16] {'z'}, dimensions={0} | all-to-all | bytes 131072 | tf_op jit(solution)/shard_map/all_to_all | solution.py:20
  105.3 14.4 %all_to_all.42 = f32[16,8,128]{2,1,0:T(8,128)S(1)} all-to-all(f32[16,8,128]{2,1,0:T(8,128)S(1)} %broadcast_in_dim.7), channel_id=1, replica_groups=mesh['x'=4,'y'=4,'core'=2,'z'=16] {'z'}, dimensions={0} | all-to-all | bytes 131072 | tf_op jit(solution)/shard_map/all_to_all | solution.py:20
  119.8 15.1 %all_to_all.43 = f32[16,128,128]{2,1,0:T(8,128)S(1)} all-to-all(f32[16,128,128]{2,1,0:T(8,128)S(1)} %broadcast_in_dim.17), channel_id=1, replica_groups=mesh['x'=4,'y'=4,'core'=2,'z'=16] {'x','y'}, dimensions={0} | all-to-all | bytes 2097152 | tf_op jit(solution)/shard_map/all_to_all | solution.py:20
  134.9 0.8 shard_map.91.factor_ref
  135.7 1.9 %shard_map.92 = f32[3584,128]{1,0:T(8,128)} custom-call(bf16[7168,256]{1,0:T(8,128)(2,1)S(1)} %copy-done, f32[256,128]{1,0:T(8,128)S(1)} %shard_map.91.factor_ref), custom_call_target="tpu_custom_call" | custom-call | tf_op jit(solution)/shard_map/pallas_call | solution.py:401
  137.6 3.9 %all-to-all-start.6 = ((f32[16,224,128]{2,1,0:T(8,128)}), f32[16,224,128]{2,1,0:T(8,128)S(1)}, u32[]{:S(2)}, u32[]{:S(2)}) async-start(f32[16,224,128]{2,1,0:T(8,128)} %bitcast.18), calls=%async_computation.6 | async-start | bytes 3670016 | tf_op jit(solution)/shard_map/all_to_all | solution.py:20
  141.5 1.9 convolution_bitcast_fusion
  143.5 5.9 %cholesky.14 = f32[64,64]{1,0:T(8,128)S(1)} custom-call(f32[64,64]{1,0:T(8,128)S(1)} %slice_add_fusion), custom_call_target="Cholesky" | custom-call | tf_op jit(solution)/shard_map/jit(cholesky)/cholesky | solution.py:486
  150.6 4.9 %custom-call.6 = f32[1,64,64]{1,2,0:T(8,128)S(1)} custom-call(f32[1,64,64]{2,1,0:T(8,128)S(1)} %fusion), custom_call_target="InvertDiagBlocksLowerTriangular" | custom-call | tf_op jit(solution)/shard_map/triangular_solve | solution.py:487
  155.7 2.4 %all-to-all-done.6.parts_ref = f32[16,224,128]{2,1,0:T(8,128)S(1)} async-done(((f32[16,224,128]{2,1,0:T(8,128)}), f32[16,224,128]{2,1,0:T(8,128)S(1)}, u32[]{:S(2)}, u32[]{:S(2)}) %all-to-all-start.6) | async-done | bytes 1835040 | tf_op jit(solution)/shard_map/all_to_all | solution.py:20
  158.1 0.9 shard_map.93.after_ref
  158.9 13.4 %all-to-all-start.7 = ((f32[32,7,128]{2,1,0:T(8,128)}), f32[32,7,128]{2,1,0:T(8,128)S(1)}, u32[]{:S(2)}, u32[]{:S(2)}) async-start(f32[32,7,128]{2,1,0:T(8,128)} %shard_map.93.after_ref), calls=%async_computation.7 | async-start | bytes 262144 | tf_op jit(solution)/shard_map/all_to_all | solution.py:20
  172.4 2.2 %collective-permute-start.4 = (f32[72,128]{1,0:T(8,128)S(1)}, f32[72,128]{1,0:T(8,128)S(1)}, u32[]{:S(2)}, u32[]{:S(2)}) collective-permute-start(f32[72,128]{1,0:T(8,128)S(1)} %shard_map.94.mine_ref), channel_id=1, source_target_pairs={{0,16},{16,0},{1,17},{17,1},{2,18},{18,2},{3,19},{19,3},{4,20},{20... | collective-permute-start | bytes 110600 | tf_op jit(solution)/shard_map/ppermute | solution.py:29
  174.5 0.9 collective-permute-done.4.other_ref
  175.5 13.3 %all-to-all-done.7.parts_ref = f32[32,7,128]{2,1,0:T(8,128)S(1)} async-done(((f32[32,7,128]{2,1,0:T(8,128)}), f32[32,7,128]{2,1,0:T(8,128)S(1)}, u32[]{:S(2)}, u32[]{:S(2)}) %all-to-all-start.7) | async-done | bytes 114720 | tf_op jit(solution)/shard_map/all_to_all | solution.py:20
  188.8 0.9 shard_map.95
  (21 shorter events, 2.8 us)
Async XLA Ops:
  2.1 33.1 %all-to-all-start = ((f32[32,7,128]{2,1,0:T(8,128)}), f32[32,7,128]{2,1,0:T(8,128)S(1)}, u32[]{:S(2)}, u32[]{:S(2)}) async-start(f32[32,7,128]{2,1,0:T(8,128)} %shard_map.84), calls=%async_computation | async-start | bytes 262144 | tf_op jit(solution)/shard_map/all_to_all | solution.py:20
  22.5 33.5 %collective-permute-start.2 = (f32[128,3584]{1,0:T(8,128)}, f32[128,3584]{1,0:T(8,128)}, u32[]{:S(2)}, u32[]{:S(2)}) collective-permute-start(f32[128,3584]{1,0:T(8,128)} %get-tuple-element.27), channel_id=1, source_target_pairs={{0,16},{16,0},{1,17},{17,1},{2,18},{18,2},{3,19},{19,3},{4,20},{20... | collective-permute-start | bytes 5505032 | tf_op jit(solution)/shard_map/ppermute | solution.py:29
  24.6 31.4 %collective-permute-start.3 = (f32[128,3584]{1,0:T(8,128)}, f32[128,3584]{1,0:T(8,128)}, u32[]{:S(2)}, u32[]{:S(2)}) collective-permute-start(f32[128,3584]{1,0:T(8,128)} %get-tuple-element.28), channel_id=1, source_target_pairs={{0,16},{16,0},{1,17},{17,1},{2,18},{18,2},{3,19},{19,3},{4,20},{20... | collective-permute-start | bytes 5505032 | tf_op jit(solution)/shard_map/ppermute | solution.py:29
  36.7 28.0 %all-to-all-start.1 = ((f32[16,224,128]{2,1,0:T(8,128)}), f32[16,224,128]{2,1,0:T(8,128)S(1)}, u32[]{:S(2)}, u32[]{:S(2)}) async-start(f32[16,224,128]{2,1,0:T(8,128)} %get-tuple-element.37), calls=%async_computation.1 | async-start | bytes 3670016 | tf_op jit(solution)/shard_map/all_to_all | solution.py:20
  48.0 5.7 %collective-permute-start = (f32[128,2048]{1,0:T(8,128)S(1)}, f32[128,2048]{1,0:T(8,128)S(1)}, u32[]{:S(2)}, u32[]{:S(2)}) collective-permute-start(f32[128,2048]{1,0:T(8,128)S(1)} %get-tuple-element.25), channel_id=1, source_target_pairs={{0,16},{16,0},{1,17},{17,1},{2,18},{18,2},{3,19},{19,3},{4,20},{20... | collective-permute-start | bytes 3145736 | tf_op jit(solution)/shard_map/ppermute | solution.py:29
  51.5 4.6 %collective-permute-start.1 = (f32[128,2048]{1,0:T(8,128)S(1)}, f32[128,2048]{1,0:T(8,128)S(1)}, u32[]{:S(2)}, u32[]{:S(2)}) collective-permute-start(f32[128,2048]{1,0:T(8,128)S(1)} %get-tuple-element.26), channel_id=1, source_target_pairs={{0,16},{16,0},{1,17},{17,1},{2,18},{18,2},{3,19},{19,3},{4,20},{20... | collective-permute-start | bytes 3145736 | tf_op jit(solution)/shard_map/ppermute | solution.py:29
  64.7 3.1 %copy-start.2 = (bf16[4096,256]{1,0:T(8,128)(2,1)S(1)}, bf16[4096,256]{1,0:T(8,128)(2,1)}, u32[]{:S(2)}) copy-start(bf16[4096,256]{1,0:T(8,128)(2,1)} %get-tuple-element.35.turned_ref) | copy-start | bytes 6291460
  90.5 44.3 %copy-start.1 = (bf16[256,4096]{1,0:T(8,128)(2,1)S(1)}, bf16[256,4096]{1,0:T(8,128)(2,1)}, u32[]{:S(2)}) copy-start(bf16[256,4096]{1,0:T(8,128)(2,1)} %get-tuple-element.34.rows_ref) | copy-start | bytes 6291460
  119.8 15.9 %copy-start = (bf16[7168,256]{1,0:T(8,128)(2,1)S(1)}, bf16[7168,256]{1,0:T(8,128)(2,1)}, u32[]{:S(2)}) copy-start(bf16[7168,256]{1,0:T(8,128)(2,1)} %get-tuple-element.33.turned_ref) | copy-start | bytes 11010052
  137.6 20.5 %all-to-all-start.6 = ((f32[16,224,128]{2,1,0:T(8,128)}), f32[16,224,128]{2,1,0:T(8,128)S(1)}, u32[]{:S(2)}, u32[]{:S(2)}) async-start(f32[16,224,128]{2,1,0:T(8,128)} %bitcast.18), calls=%async_computation.6 | async-start | bytes 3670016 | tf_op jit(solution)/shard_map/all_to_all | solution.py:20
  158.9 29.8 %all-to-all-start.7 = ((f32[32,7,128]{2,1,0:T(8,128)}), f32[32,7,128]{2,1,0:T(8,128)S(1)}, u32[]{:S(2)}, u32[]{:S(2)}) async-start(f32[32,7,128]{2,1,0:T(8,128)} %shard_map.93.after_ref), calls=%async_computation.7 | async-start | bytes 262144 | tf_op jit(solution)/shard_map/all_to_all | solution.py:20
  172.4 3.1 %collective-permute-start.4 = (f32[72,128]{1,0:T(8,128)S(1)}, f32[72,128]{1,0:T(8,128)S(1)}, u32[]{:S(2)}, u32[]{:S(2)}) collective-permute-start(f32[72,128]{1,0:T(8,128)S(1)} %shard_map.94.mine_ref), channel_id=1, source_target_pairs={{0,16},{16,0},{1,17},{17,1},{2,18},{18,2},{3,19},{19,3},{4,20},{20... | collective-permute-start | bytes 110600 | tf_op jit(solution)/shard_map/ppermute | solution.py:29

commit v5 on v4

--- a/solution.py
+++ b/solution.py
@@ -12,6 +12,7 @@
 PLANE = ("x", "y")
 LINE = ("core", "z")
 EVERY = ("x", "y", "core", "z")
+SPARE = 8
 PARAMS = pltpu.CompilerParams(vmem_limit_bytes=40 * 1024 * 1024)
 LIGHT = pl.CostEstimate(flops=1, bytes_accessed=1, transcendentals=0)
 
@@ -64,7 +65,8 @@
     half = gate_ref.shape[0] // 2
     size = out_ref.shape[0] // 2
     for which, ref in enumerate((gate_ref, up_ref)):
-        message = jnp.concatenate([ref[:half, :], ref[half:, :]], axis=1)
+        value = ref[...]
+        message = jnp.concatenate([value[:half, :], value[half:, :]], axis=1)
         for z in range(size):
             out_ref[which * size + z] = message
 
@@ -91,7 +93,7 @@
 
 def sum_kernel(parts_ref, after_ref, out_ref, line_ref):
     del after_ref
-    line_ref[...] = jnp.sum(parts_ref[...], axis=0)
+    line_ref[: parts_ref.shape[1], :] = jnp.sum(parts_ref[...], axis=0)
     size, half = out_ref.shape[0] // 2, out_ref.shape[1]
     rank = out_ref.shape[2] // 2
     for which in range(2):
@@ -114,7 +116,7 @@
         sum_kernel,
         pltpu.VMEM((2 * size, rows // (2 * size), columns), parts.dtype),
         [pltpu.VMEM, pl.ANY],
-        [pltpu.VMEM((rows, columns), parts.dtype)],
+        [pltpu.VMEM((rows + SPARE, columns), parts.dtype)],
     )(parts, after)
 
 
@@ -200,8 +202,10 @@
 def keep_kernel(count, got_ref, act_ref, gate_ref, lines_out, *refs):
     outs, scratch, (line_ref, line_sem) = refs[:4], refs[4:-2], refs[-2:]
     write_line(got_ref, line_ref)
+    rows = pl.ds(0, lines_out.shape[1])
     copies = [
-        pltpu.make_async_copy(line_ref, lines_out.at[i], line_sem.at[i]) for i in range(count)
+        pltpu.make_async_copy(line_ref.at[rows, :], lines_out.at[i], line_sem.at[i])
+        for i in range(count)
     ]
     for copy in copies:
         copy.start()
@@ -293,7 +297,7 @@
         functools.partial(keep_kernel, count),
         [pltpu.HBM((count, *line), got.dtype), *wholes],
         [pltpu.VMEM, pl.ANY, pl.ANY],
-        [*scratch, pltpu.VMEM(line, got.dtype), pltpu.SemaphoreType.DMA((count,))],
+        [*scratch, pltpu.VMEM((line[0] + SPARE, line[1]), got.dtype), pltpu.SemaphoreType.DMA((count,))],
         light=True,
     )(got, *in_hbm(act, gate))
 

time: 190 us -> 190 us (level)
  no operation moved by 1% of the time
where the time goes in v5:
time: 190 us
  blocking collectives  66.1 us (35%)
  starting transfers between devices  52.7 us (28%)
  waiting for transfers between devices  31.2 us (16%)
  Pallas kernels  24.5 us (13%)
  other arithmetic  12.2 us (6%)
  matrix products  2.03 us (1%)
    all_to_all x4, blocking collectives, exchange(): return lax.all_to_all(value, axes, 0, 0, tiled=True)  66.1 us
    all_to_all x4, starting transfers between devices, exchange(): return lax.all_to_all(value, axes, 0, 0, tiled=True)  40.8 us
    all_to_all x4, waiting for transfers between devices, exchange(): return lax.all_to_all(value, axes, 0, 0, tiled=True)  27.6 us
    ppermute x5, starting transfers between devices, other_core(): return lax.ppermute(value, 'core', [(0, 1), (1, 0)])  11.8 us
    another operation x3, other arithmetic, shards(): lower = jnp.linalg.cholesky(gram, symmetrize_input=False)  6.52 us
    another operation x2, other arithmetic, shards(): lax.linalg.triangular_solve(lower, jnp.eye(rank, dtype=jnp.float32), left...  5.55 us
    pallas_call x1, Pallas kernels, chip_arrays(): call(merge_kernel, wholes, [pl.ANY] * 8, [*[pltpu.VMEM(t.shape, t.dtype)...  5.07 us
    pallas_call x1, Pallas kernels, chip_arrays(): call(functools.partial(keep_late_kernel, count), [*wholes, half, half], [...  4.5 us
  transfers between devices with their start and end apart: 9, of which 7 were waited for; matrix products, arithmetic and copies ran while one was open for 7% of the time, Pallas kernels for 8%

profile of v5, /device:TPU:1, one launch (start us, length us, event | category | flops | bytes accessed | tf_op | source)
XLA Modules:
  0.0 189.7 jit_solution(15883435640579210370)
XLA Ops:
  0.6 1.4 shard_map.84
  2.1 16.8 %all-to-all-start = ((f32[32,7,128]{2,1,0:T(8,128)}), f32[32,7,128]{2,1,0:T(8,128)S(1)}, u32[]{:S(2)}, u32[]{:S(2)}) async-start(f32[32,7,128]{2,1,0:T(8,128)} %shard_map.84), calls=%async_computation | async-start | bytes 262144 | tf_op jit(solution)/shard_map/all_to_all | solution.py:21
  18.8 3.6 %shard_map.87 = (f32[128,3584]{1,0:T(8,128)}, f32[128,3584]{1,0:T(8,128)}) custom-call(bf16[128,7168]{1,0:T(8,128)(2,1)} %gate_ref.5, bf16[128,7168]{1,0:T(8,128)(2,1)} %up_ref.5), custom_call_target="tpu_custom_call" | custom-call | flops 1 | bytes 1 | tf_op jit(solution)/shard_map/pallas_call | solution.py:157
  22.5 2.1 %collective-permute-start.2 = (f32[128,3584]{1,0:T(8,128)}, f32[128,3584]{1,0:T(8,128)}, u32[]{:S(2)}, u32[]{:S(2)}) collective-permute-start(f32[128,3584]{1,0:T(8,128)} %get-tuple-element.27), channel_id=1, source_target_pairs={{0,16},{16,0},{1,17},{17,1},{2,18},{18,2},{3,19},{19,3},{4,20},{20... | collective-permute-start | bytes 5505032 | tf_op jit(solution)/shard_map/ppermute | solution.py:30
  24.6 2.2 %collective-permute-start.3 = (f32[128,3584]{1,0:T(8,128)}, f32[128,3584]{1,0:T(8,128)}, u32[]{:S(2)}, u32[]{:S(2)}) collective-permute-start(f32[128,3584]{1,0:T(8,128)} %get-tuple-element.28), channel_id=1, source_target_pairs={{0,16},{16,0},{1,17},{17,1},{2,18},{18,2},{3,19},{19,3},{4,20},{20... | collective-permute-start | bytes 5505032 | tf_op jit(solution)/shard_map/ppermute | solution.py:30
  26.8 8.4 %all-to-all-done.got_ref = f32[32,7,128]{2,1,0:T(8,128)S(1)} async-done(((f32[32,7,128]{2,1,0:T(8,128)}), f32[32,7,128]{2,1,0:T(8,128)S(1)}, u32[]{:S(2)}, u32[]{:S(2)}) %all-to-all-start) | async-done | bytes 114720 | tf_op jit(solution)/shard_map/all_to_all | solution.py:21
  35.2 1.5 shard_map.85
  36.8 6.8 %all-to-all-start.1 = ((f32[16,224,128]{2,1,0:T(8,128)}), f32[16,224,128]{2,1,0:T(8,128)S(1)}, u32[]{:S(2)}, u32[]{:S(2)}) async-start(f32[16,224,128]{2,1,0:T(8,128)} %get-tuple-element.37), calls=%async_computation.1 | async-start | bytes 3670016 | tf_op jit(solution)/shard_map/all_to_all | solution.py:21
  43.5 4.5 %shard_map.86 = (bf16[256,4096]{1,0:T(8,128)(2,1)}, bf16[4096,256]{1,0:T(8,128)(2,1)}, bf16[256,7168]{1,0:T(8,128)(2,1)}, bf16[7168,256]{1,0:T(8,128)(2,1)}, f32...) custom-call(bf16[128,4096]{1,0:T(8,128)(2,1)} %act_ref.3, ...), custom_call_target="tpu_custom_call", output_to_operand_aliasing={{0}: (2, {}), {1}: (3, {}), {2}: (4, {}), {3}: (5, {})} | custom-call | flops 1 | bytes 1 | tf_op jit(solution)/shard_map/pallas_call | solution.py:305
  48.0 3.4 %collective-permute-start = (f32[128,2048]{1,0:T(8,128)S(1)}, f32[128,2048]{1,0:T(8,128)S(1)}, u32[]{:S(2)}, u32[]{:S(2)}) collective-permute-start(f32[128,2048]{1,0:T(8,128)S(1)} %get-tuple-element.25), channel_id=1, source_target_pairs={{0,16},{16,0},{1,17},{17,1},{2,18},{18,2},{3,19},{19,3},{4,20},{20... | collective-permute-start | bytes 3145736 | tf_op jit(solution)/shard_map/ppermute | solution.py:30
  51.5 1.9 %collective-permute-start.1 = (f32[128,2048]{1,0:T(8,128)S(1)}, f32[128,2048]{1,0:T(8,128)S(1)}, u32[]{:S(2)}, u32[]{:S(2)}) collective-permute-start(f32[128,2048]{1,0:T(8,128)S(1)} %get-tuple-element.26), channel_id=1, source_target_pairs={{0,16},{16,0},{1,17},{17,1},{2,18},{18,2},{3,19},{19,3},{4,20},{20... | collective-permute-start | bytes 3145736 | tf_op jit(solution)/shard_map/ppermute | solution.py:30
  53.7 2.3 %collective-permute-done.1.refs_1_ = f32[128,2048]{1,0:T(8,128)S(1)} collective-permute-done((f32[128,2048]{1,0:T(8,128)S(1)}, f32[128,2048]{1,0:T(8,128)S(1)}, u32[]{:S(2)}, u32[]{:S(2)}) %collective-permute-start.1) | collective-permute-done | bytes 1048608 | tf_op jit(solution)/shard_map/ppermute | solution.py:30
  56.0 5.1 %shard_map.88 = (bf16[256,4096]{1,0:T(8,128)(2,1)}, bf16[4096,256]{1,0:T(8,128)(2,1)}, bf16[256,7168]{1,0:T(8,128)(2,1)}, bf16[7168,256]{1,0:T(8,128)(2,1)}) custom-call(f32[128,2048]{1,0:T(8,128)S(1)} %collective-permute-done.refs_0_, ...), custom_call_target="tpu_custom_call", output_to_operand_aliasing={{0}: (4, {}), {1}: (5, {}), {2}: (6, {}), {3}: (7, {})} | custom-call | flops 1 | bytes 1 | tf_op jit(solution)/shard_map/pallas_call | solution.py:316
  61.1 3.6 %all-to-all-done.1 = f32[16,224,128]{2,1,0:T(8,128)S(1)} async-done(((f32[16,224,128]{2,1,0:T(8,128)}), f32[16,224,128]{2,1,0:T(8,128)S(1)}, u32[]{:S(2)}, u32[]{:S(2)}) %all-to-all-start.1) | async-done | bytes 1835040 | tf_op jit(solution)/shard_map/all_to_all | solution.py:21
  64.7 3.1 %shard_map.89.factor_ref = f32[256,128]{1,0:T(8,128)S(1)} custom-call(bf16[256,7168]{1,0:T(8,128)(2,1)} %get-tuple-element.36.grad_ref, f32[3584,128]{1,0:T(8,128)S(1)} %bitcast.16), custom_call_target="tpu_custom_call" | custom-call | tf_op jit(solution)/shard_map/pallas_call | solution.py:471
  68.6 22.0 %all_to_all.40 = f32[16,128,128]{2,1,0:T(8,128)S(1)} all-to-all(f32[16,128,128]{2,1,0:T(8,128)S(1)} %bitcast.17), channel_id=1, replica_groups=mesh['x'=4,'y'=4,'core'=2,'z'=16] {'x','y'}, dimensions={0} | all-to-all | bytes 2097152 | tf_op jit(solution)/shard_map/all_to_all | solution.py:21
  90.6 14.6 %all_to_all.41 = f32[16,8,128]{2,1,0:T(8,128)S(1)} all-to-all(f32[16,8,128]{2,1,0:T(8,128)S(1)} %bitcast.19), channel_id=1, replica_groups=mesh['x'=4,'y'=4,'core'=2,'z'=16] {'z'}, dimensions={0} | all-to-all | bytes 131072 | tf_op jit(solution)/shard_map/all_to_all | solution.py:21
  105.2 14.4 %all_to_all.42 = f32[16,8,128]{2,1,0:T(8,128)S(1)} all-to-all(f32[16,8,128]{2,1,0:T(8,128)S(1)} %broadcast_in_dim.7), channel_id=1, replica_groups=mesh['x'=4,'y'=4,'core'=2,'z'=16] {'z'}, dimensions={0} | all-to-all | bytes 131072 | tf_op jit(solution)/shard_map/all_to_all | solution.py:21
  119.8 15.1 %all_to_all.43 = f32[16,128,128]{2,1,0:T(8,128)S(1)} all-to-all(f32[16,128,128]{2,1,0:T(8,128)S(1)} %broadcast_in_dim.17), channel_id=1, replica_groups=mesh['x'=4,'y'=4,'core'=2,'z'=16] {'x','y'}, dimensions={0} | all-to-all | bytes 2097152 | tf_op jit(solution)/shard_map/all_to_all | solution.py:21
  134.8 0.8 shard_map.91.factor_ref
  135.7 1.9 %shard_map.92 = f32[3584,128]{1,0:T(8,128)} custom-call(bf16[7168,256]{1,0:T(8,128)(2,1)S(1)} %copy-done, f32[256,128]{1,0:T(8,128)S(1)} %shard_map.91.factor_ref), custom_call_target="tpu_custom_call" | custom-call | tf_op jit(solution)/shard_map/pallas_call | solution.py:405
  137.6 3.9 %all-to-all-start.6 = ((f32[16,224,128]{2,1,0:T(8,128)}), f32[16,224,128]{2,1,0:T(8,128)S(1)}, u32[]{:S(2)}, u32[]{:S(2)}) async-start(f32[16,224,128]{2,1,0:T(8,128)} %bitcast.18), calls=%async_computation.6 | async-start | bytes 3670016 | tf_op jit(solution)/shard_map/all_to_all | solution.py:21
  141.5 1.9 convolution_bitcast_fusion
  143.4 5.9 %cholesky.14 = f32[64,64]{1,0:T(8,128)S(1)} custom-call(f32[64,64]{1,0:T(8,128)S(1)} %slice_add_fusion), custom_call_target="Cholesky" | custom-call | tf_op jit(solution)/shard_map/jit(cholesky)/cholesky | solution.py:490
  150.6 4.9 %custom-call.6 = f32[1,64,64]{1,2,0:T(8,128)S(1)} custom-call(f32[1,64,64]{2,1,0:T(8,128)S(1)} %fusion), custom_call_target="InvertDiagBlocksLowerTriangular" | custom-call | tf_op jit(solution)/shard_map/triangular_solve | solution.py:491
  155.7 2.4 %all-to-all-done.6.parts_ref = f32[16,224,128]{2,1,0:T(8,128)S(1)} async-done(((f32[16,224,128]{2,1,0:T(8,128)}), f32[16,224,128]{2,1,0:T(8,128)S(1)}, u32[]{:S(2)}, u32[]{:S(2)}) %all-to-all-start.6) | async-done | bytes 1835040 | tf_op jit(solution)/shard_map/all_to_all | solution.py:21
  158.1 0.9 shard_map.93.after_ref
  158.9 13.4 %all-to-all-start.7 = ((f32[32,7,128]{2,1,0:T(8,128)}), f32[32,7,128]{2,1,0:T(8,128)S(1)}, u32[]{:S(2)}, u32[]{:S(2)}) async-start(f32[32,7,128]{2,1,0:T(8,128)} %shard_map.93.after_ref), calls=%async_computation.7 | async-start | bytes 262144 | tf_op jit(solution)/shard_map/all_to_all | solution.py:21
  172.3 2.2 %collective-permute-start.4 = (f32[72,128]{1,0:T(8,128)S(1)}, f32[72,128]{1,0:T(8,128)S(1)}, u32[]{:S(2)}, u32[]{:S(2)}) collective-permute-start(f32[72,128]{1,0:T(8,128)S(1)} %shard_map.94.mine_ref), channel_id=1, source_target_pairs={{0,16},{16,0},{1,17},{17,1},{2,18},{18,2},{3,19},{19,3},{4,20},{20... | collective-permute-start | bytes 110600 | tf_op jit(solution)/shard_map/ppermute | solution.py:30
  174.5 0.9 collective-permute-done.4.other_ref
  175.5 13.3 %all-to-all-done.7.parts_ref = f32[32,7,128]{2,1,0:T(8,128)S(1)} async-done(((f32[32,7,128]{2,1,0:T(8,128)}), f32[32,7,128]{2,1,0:T(8,128)S(1)}, u32[]{:S(2)}, u32[]{:S(2)}) %all-to-all-start.7) | async-done | bytes 114720 | tf_op jit(solution)/shard_map/all_to_all | solution.py:21
  188.8 0.9 shard_map.95
  (21 shorter events, 2.8 us)
Async XLA Ops:
  2.1 33.1 %all-to-all-start = ((f32[32,7,128]{2,1,0:T(8,128)}), f32[32,7,128]{2,1,0:T(8,128)S(1)}, u32[]{:S(2)}, u32[]{:S(2)}) async-start(f32[32,7,128]{2,1,0:T(8,128)} %shard_map.84), calls=%async_computation | async-start | bytes 262144 | tf_op jit(solution)/shard_map/all_to_all | solution.py:21
  22.5 33.5 %collective-permute-start.2 = (f32[128,3584]{1,0:T(8,128)}, f32[128,3584]{1,0:T(8,128)}, u32[]{:S(2)}, u32[]{:S(2)}) collective-permute-start(f32[128,3584]{1,0:T(8,128)} %get-tuple-element.27), channel_id=1, source_target_pairs={{0,16},{16,0},{1,17},{17,1},{2,18},{18,2},{3,19},{19,3},{4,20},{20... | collective-permute-start | bytes 5505032 | tf_op jit(solution)/shard_map/ppermute | solution.py:30
  24.6 31.4 %collective-permute-start.3 = (f32[128,3584]{1,0:T(8,128)}, f32[128,3584]{1,0:T(8,128)}, u32[]{:S(2)}, u32[]{:S(2)}) collective-permute-start(f32[128,3584]{1,0:T(8,128)} %get-tuple-element.28), channel_id=1, source_target_pairs={{0,16},{16,0},{1,17},{17,1},{2,18},{18,2},{3,19},{19,3},{4,20},{20... | collective-permute-start | bytes 5505032 | tf_op jit(solution)/shard_map/ppermute | solution.py:30
  36.8 28.0 %all-to-all-start.1 = ((f32[16,224,128]{2,1,0:T(8,128)}), f32[16,224,128]{2,1,0:T(8,128)S(1)}, u32[]{:S(2)}, u32[]{:S(2)}) async-start(f32[16,224,128]{2,1,0:T(8,128)} %get-tuple-element.37), calls=%async_computation.1 | async-start | bytes 3670016 | tf_op jit(solution)/shard_map/all_to_all | solution.py:21
  48.0 5.7 %collective-permute-start = (f32[128,2048]{1,0:T(8,128)S(1)}, f32[128,2048]{1,0:T(8,128)S(1)}, u32[]{:S(2)}, u32[]{:S(2)}) collective-permute-start(f32[128,2048]{1,0:T(8,128)S(1)} %get-tuple-element.25), channel_id=1, source_target_pairs={{0,16},{16,0},{1,17},{17,1},{2,18},{18,2},{3,19},{19,3},{4,20},{20... | collective-permute-start | bytes 3145736 | tf_op jit(solution)/shard_map/ppermute | solution.py:30
  51.5 4.6 %collective-permute-start.1 = (f32[128,2048]{1,0:T(8,128)S(1)}, f32[128,2048]{1,0:T(8,128)S(1)}, u32[]{:S(2)}, u32[]{:S(2)}) collective-permute-start(f32[128,2048]{1,0:T(8,128)S(1)} %get-tuple-element.26), channel_id=1, source_target_pairs={{0,16},{16,0},{1,17},{17,1},{2,18},{18,2},{3,19},{19,3},{4,20},{20... | collective-permute-start | bytes 3145736 | tf_op jit(solution)/shard_map/ppermute | solution.py:30
  64.7 3.1 %copy-start.2 = (bf16[4096,256]{1,0:T(8,128)(2,1)S(1)}, bf16[4096,256]{1,0:T(8,128)(2,1)}, u32[]{:S(2)}) copy-start(bf16[4096,256]{1,0:T(8,128)(2,1)} %get-tuple-element.35.turned_ref) | copy-start | bytes 6291460
  90.5 44.3 %copy-start.1 = (bf16[256,4096]{1,0:T(8,128)(2,1)S(1)}, bf16[256,4096]{1,0:T(8,128)(2,1)}, u32[]{:S(2)}) copy-start(bf16[256,4096]{1,0:T(8,128)(2,1)} %get-tuple-element.34.rows_ref) | copy-start | bytes 6291460
  119.7 15.9 %copy-start = (bf16[7168,256]{1,0:T(8,128)(2,1)S(1)}, bf16[7168,256]{1,0:T(8,128)(2,1)}, u32[]{:S(2)}) copy-start(bf16[7168,256]{1,0:T(8,128)(2,1)} %get-tuple-element.33.turned_ref) | copy-start | bytes 11010052
  137.6 20.5 %all-to-all-start.6 = ((f32[16,224,128]{2,1,0:T(8,128)}), f32[16,224,128]{2,1,0:T(8,128)S(1)}, u32[]{:S(2)}, u32[]{:S(2)}) async-start(f32[16,224,128]{2,1,0:T(8,128)} %bitcast.18), calls=%async_computation.6 | async-start | bytes 3670016 | tf_op jit(solution)/shard_map/all_to_all | solution.py:21
  158.9 29.9 %all-to-all-start.7 = ((f32[32,7,128]{2,1,0:T(8,128)}), f32[32,7,128]{2,1,0:T(8,128)S(1)}, u32[]{:S(2)}, u32[]{:S(2)}) async-start(f32[32,7,128]{2,1,0:T(8,128)} %shard_map.93.after_ref), calls=%async_computation.7 | async-start | bytes 262144 | tf_op jit(solution)/shard_map/all_to_all | solution.py:21
  172.3 3.1 %collective-permute-start.4 = (f32[72,128]{1,0:T(8,128)S(1)}, f32[72,128]{1,0:T(8,128)S(1)}, u32[]{:S(2)}, u32[]{:S(2)}) collective-permute-start(f32[72,128]{1,0:T(8,128)S(1)} %shard_map.94.mine_ref), channel_id=1, source_target_pairs={{0,16},{16,0},{1,17},{17,1},{2,18},{18,2},{3,19},{19,3},{4,20},{20... | collective-permute-start | bytes 110600 | tf_op jit(solution)/shard_map/ppermute | solution.py:30
